TPU v7x, 32 devices: a whole 2x2x4 slice. The times are simulated.
32 devices in a mesh: band: 4 (over x, core), feed: 8 (over z, y).
Axes of the slice: x: 2, y: 2, z: 4, core: 2. Of those that a mesh axis runs over, the one named last changes fastest.
Arguments:
- voltages: float32 [768, 2048, 128], P('band', 'feed'), may hold values from -6 to 6
- feed_cells: int32 [4096], replicated, may hold values from 0 to 4095, each once
- delays: int32 [768, 256], P('band'), may hold values from 0 to 63
Outputs:
- dedispersed: float32 [256, 1024, 64], P('band', 'feed')
Inputs may be any that keep to these rules, and one draw needn't show every extreme that they name: `feed_cells`: a permutation of the cells of the 64 x 64 feed grid, so no two feeds share a cell.
All inputs are finite; a program needn't handle non-finite values.
Results may differ from a plain program's by a relative error of at most 0.0003.
Values sent between devices are 32-bit elements; how exact they have to be, the bound alone decides.
No kernel may reach another device: no remote copies, remote signals or barrier semaphores. Data moves between devices by JAX's collectives and lax.ppermute only.
A program may use at most 128 MiB of HBM per device.

v0:
```python
import math

import jax
import jax.numpy as jnp
from jax import lax
from jax.sharding import PartitionSpec as P

FEEDS = 2048
CHANNELS = 768
FRAMES = 64
SIDE = 32
BEAMS = 1024
GRID = 64


def feed_offsets(feed_cells):
    cell_index = feed_cells[:FEEDS]
    cell_row = cell_index // GRID
    cell_col = cell_index % GRID
    beam_ids = jnp.arange(BEAMS, dtype=jnp.int32)
    beam_row = beam_ids // SIDE - SIDE // 2
    beam_col = beam_ids % SIDE - SIDE // 2
    return beam_row[:, None] * cell_row[None, :] + beam_col[:, None] * cell_col[None, :]


def steering(offsets, channel):
    residue = jnp.mod(offsets * (CHANNELS + channel), GRID * CHANNELS)
    phases = residue.astype(jnp.float32) * (2.0 * math.pi / (GRID * CHANNELS))
    factor = 1.0 / math.sqrt(FEEDS)
    return (jnp.cos(phases) * factor, jnp.sin(phases) * factor)


def frame_tables():
    frame_ids = jnp.arange(FRAMES, dtype=jnp.int32)
    wave = jnp.mod(frame_ids[:, None] * frame_ids[None, :], FRAMES).astype(jnp.float32) * (
        2.0 * math.pi / FRAMES
    )
    nonzero = (frame_ids > 0).astype(jnp.float32)[None, :]
    forward = jnp.concatenate([jnp.cos(wave) * nonzero, -jnp.sin(wave) * nonzero], axis=1)
    inverse = jnp.concatenate([jnp.cos(wave), -jnp.sin(wave)], axis=0) * (
        0.5 / (FRAMES * math.sqrt(CHANNELS))
    )
    return (frame_ids, forward, inverse)


def to_spectra(by_beam, chan_count, forward):
    beams_here = by_beam.shape[1] // FRAMES
    spectra = jnp.dot(
        by_beam.reshape(chan_count * beams_here, FRAMES), forward, precision=lax.Precision.HIGHEST
    )
    spectra = spectra.reshape(chan_count, beams_here, 2 * FRAMES)
    return (spectra[:, :, :FRAMES], spectra[:, :, FRAMES:])


def shifted_rows(spec_real, spec_imag, table, frame_ids):
    highest = lax.Precision.HIGHEST
    residue = jnp.mod(frame_ids[:, None, None] * table[None, :, :], FRAMES)
    phases = residue.astype(jnp.float32) * (2.0 * math.pi / FRAMES)
    shift_cos = jnp.cos(phases)
    shift_sin = jnp.sin(phases)
    out_real = jnp.einsum("kcd,cbk->dbk", shift_cos, spec_real, precision=highest)
    out_real = out_real - jnp.einsum("kcd,cbk->dbk", shift_sin, spec_imag, precision=highest)
    out_imag = jnp.einsum("kcd,cbk->dbk", shift_cos, spec_imag, precision=highest)
    out_imag = out_imag + jnp.einsum("kcd,cbk->dbk", shift_sin, spec_real, precision=highest)
    return jnp.concatenate([out_real, out_imag], axis=2)


def to_series(folded, inverse):
    row_count, beams_here = (folded.shape[0], folded.shape[1])
    series = jnp.dot(
        folded.reshape(row_count * beams_here, 2 * FRAMES), inverse, precision=lax.Precision.HIGHEST
    )
    return series.reshape(row_count, beams_here, FRAMES)


def body(voltages, feed_cells, delays):
    highest = lax.Precision.HIGHEST
    band_chans = voltages.shape[0]
    by_channel = lax.all_to_all(voltages, "feed", split_axis=0, concat_axis=1, tiled=True)
    local_chans = by_channel.shape[0]
    first_chan = lax.axis_index("band") * band_chans + lax.axis_index("feed") * local_chans
    offsets = feed_offsets(feed_cells)

    def beam_power(item):
        channel, voltage = item
        cosine, sine_part = steering(offsets, channel)
        weights = jnp.concatenate([cosine, sine_part], axis=0)
        products = jnp.dot(weights, voltage, precision=highest)
        with_cos = products[:BEAMS]
        with_sin = products[BEAMS:]
        real_part = with_cos[:, :FRAMES] + with_sin[:, FRAMES:]
        imag_part = with_cos[:, FRAMES:] - with_sin[:, :FRAMES]
        return (real_part * real_part + imag_part * imag_part).reshape(BEAMS * FRAMES)

    channels = first_chan + jnp.arange(local_chans, dtype=jnp.int32)
    powers = lax.map(beam_power, (channels, by_channel))
    frame_ids, forward, inverse = frame_tables()
    by_beam = lax.all_to_all(powers, "feed", split_axis=1, concat_axis=0, tiled=True)
    spec_real, spec_imag = to_spectra(by_beam, band_chans, forward)
    return lax.psum_scatter(
        to_series(shifted_rows(spec_real, spec_imag, delays, frame_ids), inverse),
        "band",
        scatter_dimension=0,
        tiled=True,
    )


def solution(mesh):
    placed = (P("band", "feed", None), P(), P("band", None))
    return jax.shard_map(
        body, mesh=mesh, in_specs=placed, out_specs=P("band", "feed", None), check_vma=False
    )
```

profile of v0, /device:TPU:0, one launch (start us, length us, event | category | flops | bytes accessed | tf_op | source)
XLA Modules:
  0.0 2713.0 jit_solution(15303257801777547770)
XLA Ops:
  14.0 543.9 %all-to-all-done = f32[192,256,128]{2,1,0:T(8,128)} async-done(((f32[192,256,128]{2,1,0:T(8,128)}), f32[192,256,128]{2,1,0:T(8,128)}, u32[]{:S(2)}, u32[]{:S(2)}) %all-to-all-start) | async-done | bytes 25165856 | tf_op jit(solution)/shard_map/all_to_all | solution.py:79
  575.2 1576.4 %while.13 = (s32[]{:T(128)}, f32[24,65536]{1,0:T(8,128)}, s32[24]{0:T(128)S(1)}, f32[24,2048,128]{2,1,0:T(8,128)}, s32[2048]{0:T(1024)S(1)}, /*index=5*/s32[1024...) while((s32[]{:T(128)}, f32[24,65536]{1,0:T(8,128)}, ...), condition=%wide.region_1.2_spmd.clone, body=%wide.region_0.1_spmd.clone.sunk | while | flops 6476333056 | bytes 38559896 | solution.py:96
  576.3 36.8 %cosine_multiply_fusion.2 = (f32[1024,2048]{1,0:T(8,128)S(1)}, f32[1024,2048]{1,0:T(8,128)}) fusion(s32[]{:T(128)} %bitcast.30, s32[2048]{0:T(1024)S(1)} %get-tuple-element.203, s32[1024]{0:T(1024)S(1)} %get-tuple-element.204, s32[2048]{0:T(1024)S(1)} %get-tuple-element.201, s32[1024]{0:T(1024)S(1)} %get-tuple-element.202), kind=kLoop, calls=%fused_computation.13.clone.1 | loop fusion | flops 29360128 | bytes 16801796 | tf_op jit(solution)/shard_map/while/body/eval_jaxpr/mul | solution.py:30
  613.1 21.1 fusion.111
  642.0 36.8 %cosine_multiply_fusion.2 = (f32[1024,2048]{1,0:T(8,128)S(1)}, f32[1024,2048]{1,0:T(8,128)}) fusion(s32[]{:T(128)} %bitcast.30, s32[2048]{0:T(1024)S(1)} %get-tuple-element.203, s32[1024]{0:T(1024)S(1)} %get-tuple-element.204, s32[2048]{0:T(1024)S(1)} %get-tuple-element.201, s32[1024]{0:T(1024)S(1)} %get-tuple-element.202), kind=kLoop, calls=%fused_computation.13.clone.1 | loop fusion | flops 29360128 | bytes 16801796 | tf_op jit(solution)/shard_map/while/body/eval_jaxpr/mul | solution.py:30
  678.8 21.1 fusion.111
  707.6 36.8 %cosine_multiply_fusion.2 = (f32[1024,2048]{1,0:T(8,128)S(1)}, f32[1024,2048]{1,0:T(8,128)}) fusion(s32[]{:T(128)} %bitcast.30, s32[2048]{0:T(1024)S(1)} %get-tuple-element.203, s32[1024]{0:T(1024)S(1)} %get-tuple-element.204, s32[2048]{0:T(1024)S(1)} %get-tuple-element.201, s32[1024]{0:T(1024)S(1)} %get-tuple-element.202), kind=kLoop, calls=%fused_computation.13.clone.1 | loop fusion | flops 29360128 | bytes 16801796 | tf_op jit(solution)/shard_map/while/body/eval_jaxpr/mul | solution.py:30
  744.4 21.1 fusion.111
  773.3 36.8 %cosine_multiply_fusion.2 = (f32[1024,2048]{1,0:T(8,128)S(1)}, f32[1024,2048]{1,0:T(8,128)}) fusion(s32[]{:T(128)} %bitcast.30, s32[2048]{0:T(1024)S(1)} %get-tuple-element.203, s32[1024]{0:T(1024)S(1)} %get-tuple-element.204, s32[2048]{0:T(1024)S(1)} %get-tuple-element.201, s32[1024]{0:T(1024)S(1)} %get-tuple-element.202), kind=kLoop, calls=%fused_computation.13.clone.1 | loop fusion | flops 29360128 | bytes 16801796 | tf_op jit(solution)/shard_map/while/body/eval_jaxpr/mul | solution.py:30
  810.1 21.1 fusion.111
  839.0 36.8 %cosine_multiply_fusion.2 = (f32[1024,2048]{1,0:T(8,128)S(1)}, f32[1024,2048]{1,0:T(8,128)}) fusion(s32[]{:T(128)} %bitcast.30, s32[2048]{0:T(1024)S(1)} %get-tuple-element.203, s32[1024]{0:T(1024)S(1)} %get-tuple-element.204, s32[2048]{0:T(1024)S(1)} %get-tuple-element.201, s32[1024]{0:T(1024)S(1)} %get-tuple-element.202), kind=kLoop, calls=%fused_computation.13.clone.1 | loop fusion | flops 29360128 | bytes 16801796 | tf_op jit(solution)/shard_map/while/body/eval_jaxpr/mul | solution.py:30
  875.8 21.1 fusion.111
  904.6 36.8 %cosine_multiply_fusion.2 = (f32[1024,2048]{1,0:T(8,128)S(1)}, f32[1024,2048]{1,0:T(8,128)}) fusion(s32[]{:T(128)} %bitcast.30, s32[2048]{0:T(1024)S(1)} %get-tuple-element.203, s32[1024]{0:T(1024)S(1)} %get-tuple-element.204, s32[2048]{0:T(1024)S(1)} %get-tuple-element.201, s32[1024]{0:T(1024)S(1)} %get-tuple-element.202), kind=kLoop, calls=%fused_computation.13.clone.1 | loop fusion | flops 29360128 | bytes 16801796 | tf_op jit(solution)/shard_map/while/body/eval_jaxpr/mul | solution.py:30
  941.4 21.1 fusion.111
  970.3 36.8 %cosine_multiply_fusion.2 = (f32[1024,2048]{1,0:T(8,128)S(1)}, f32[1024,2048]{1,0:T(8,128)}) fusion(s32[]{:T(128)} %bitcast.30, s32[2048]{0:T(1024)S(1)} %get-tuple-element.203, s32[1024]{0:T(1024)S(1)} %get-tuple-element.204, s32[2048]{0:T(1024)S(1)} %get-tuple-element.201, s32[1024]{0:T(1024)S(1)} %get-tuple-element.202), kind=kLoop, calls=%fused_computation.13.clone.1 | loop fusion | flops 29360128 | bytes 16801796 | tf_op jit(solution)/shard_map/while/body/eval_jaxpr/mul | solution.py:30
  1007.1 21.1 fusion.111
  1036.0 36.8 %cosine_multiply_fusion.2 = (f32[1024,2048]{1,0:T(8,128)S(1)}, f32[1024,2048]{1,0:T(8,128)}) fusion(s32[]{:T(128)} %bitcast.30, s32[2048]{0:T(1024)S(1)} %get-tuple-element.203, s32[1024]{0:T(1024)S(1)} %get-tuple-element.204, s32[2048]{0:T(1024)S(1)} %get-tuple-element.201, s32[1024]{0:T(1024)S(1)} %get-tuple-element.202), kind=kLoop, calls=%fused_computation.13.clone.1 | loop fusion | flops 29360128 | bytes 16801796 | tf_op jit(solution)/shard_map/while/body/eval_jaxpr/mul | solution.py:30
  1072.8 21.1 fusion.111
  1101.6 36.8 %cosine_multiply_fusion.2 = (f32[1024,2048]{1,0:T(8,128)S(1)}, f32[1024,2048]{1,0:T(8,128)}) fusion(s32[]{:T(128)} %bitcast.30, s32[2048]{0:T(1024)S(1)} %get-tuple-element.203, s32[1024]{0:T(1024)S(1)} %get-tuple-element.204, s32[2048]{0:T(1024)S(1)} %get-tuple-element.201, s32[1024]{0:T(1024)S(1)} %get-tuple-element.202), kind=kLoop, calls=%fused_computation.13.clone.1 | loop fusion | flops 29360128 | bytes 16801796 | tf_op jit(solution)/shard_map/while/body/eval_jaxpr/mul | solution.py:30
  1138.4 21.1 fusion.111
  1167.3 36.8 %cosine_multiply_fusion.2 = (f32[1024,2048]{1,0:T(8,128)S(1)}, f32[1024,2048]{1,0:T(8,128)}) fusion(s32[]{:T(128)} %bitcast.30, s32[2048]{0:T(1024)S(1)} %get-tuple-element.203, s32[1024]{0:T(1024)S(1)} %get-tuple-element.204, s32[2048]{0:T(1024)S(1)} %get-tuple-element.201, s32[1024]{0:T(1024)S(1)} %get-tuple-element.202), kind=kLoop, calls=%fused_computation.13.clone.1 | loop fusion | flops 29360128 | bytes 16801796 | tf_op jit(solution)/shard_map/while/body/eval_jaxpr/mul | solution.py:30
  1204.1 21.1 fusion.111
  1233.0 36.8 %cosine_multiply_fusion.2 = (f32[1024,2048]{1,0:T(8,128)S(1)}, f32[1024,2048]{1,0:T(8,128)}) fusion(s32[]{:T(128)} %bitcast.30, s32[2048]{0:T(1024)S(1)} %get-tuple-element.203, s32[1024]{0:T(1024)S(1)} %get-tuple-element.204, s32[2048]{0:T(1024)S(1)} %get-tuple-element.201, s32[1024]{0:T(1024)S(1)} %get-tuple-element.202), kind=kLoop, calls=%fused_computation.13.clone.1 | loop fusion | flops 29360128 | bytes 16801796 | tf_op jit(solution)/shard_map/while/body/eval_jaxpr/mul | solution.py:30
  1269.8 21.1 fusion.111
  1298.6 36.8 %cosine_multiply_fusion.2 = (f32[1024,2048]{1,0:T(8,128)S(1)}, f32[1024,2048]{1,0:T(8,128)}) fusion(s32[]{:T(128)} %bitcast.30, s32[2048]{0:T(1024)S(1)} %get-tuple-element.203, s32[1024]{0:T(1024)S(1)} %get-tuple-element.204, s32[2048]{0:T(1024)S(1)} %get-tuple-element.201, s32[1024]{0:T(1024)S(1)} %get-tuple-element.202), kind=kLoop, calls=%fused_computation.13.clone.1 | loop fusion | flops 29360128 | bytes 16801796 | tf_op jit(solution)/shard_map/while/body/eval_jaxpr/mul | solution.py:30
  1335.4 21.1 fusion.111
  1364.3 36.8 %cosine_multiply_fusion.2 = (f32[1024,2048]{1,0:T(8,128)S(1)}, f32[1024,2048]{1,0:T(8,128)}) fusion(s32[]{:T(128)} %bitcast.30, s32[2048]{0:T(1024)S(1)} %get-tuple-element.203, s32[1024]{0:T(1024)S(1)} %get-tuple-element.204, s32[2048]{0:T(1024)S(1)} %get-tuple-element.201, s32[1024]{0:T(1024)S(1)} %get-tuple-element.202), kind=kLoop, calls=%fused_computation.13.clone.1 | loop fusion | flops 29360128 | bytes 16801796 | tf_op jit(solution)/shard_map/while/body/eval_jaxpr/mul | solution.py:30
  1401.1 21.1 fusion.111
  1430.0 36.8 %cosine_multiply_fusion.2 = (f32[1024,2048]{1,0:T(8,128)S(1)}, f32[1024,2048]{1,0:T(8,128)}) fusion(s32[]{:T(128)} %bitcast.30, s32[2048]{0:T(1024)S(1)} %get-tuple-element.203, s32[1024]{0:T(1024)S(1)} %get-tuple-element.204, s32[2048]{0:T(1024)S(1)} %get-tuple-element.201, s32[1024]{0:T(1024)S(1)} %get-tuple-element.202), kind=kLoop, calls=%fused_computation.13.clone.1 | loop fusion | flops 29360128 | bytes 16801796 | tf_op jit(solution)/shard_map/while/body/eval_jaxpr/mul | solution.py:30
  1466.8 21.1 fusion.111
  1495.6 36.8 %cosine_multiply_fusion.2 = (f32[1024,2048]{1,0:T(8,128)S(1)}, f32[1024,2048]{1,0:T(8,128)}) fusion(s32[]{:T(128)} %bitcast.30, s32[2048]{0:T(1024)S(1)} %get-tuple-element.203, s32[1024]{0:T(1024)S(1)} %get-tuple-element.204, s32[2048]{0:T(1024)S(1)} %get-tuple-element.201, s32[1024]{0:T(1024)S(1)} %get-tuple-element.202), kind=kLoop, calls=%fused_computation.13.clone.1 | loop fusion | flops 29360128 | bytes 16801796 | tf_op jit(solution)/shard_map/while/body/eval_jaxpr/mul | solution.py:30
  1532.4 21.1 fusion.111
  1561.3 36.8 %cosine_multiply_fusion.2 = (f32[1024,2048]{1,0:T(8,128)S(1)}, f32[1024,2048]{1,0:T(8,128)}) fusion(s32[]{:T(128)} %bitcast.30, s32[2048]{0:T(1024)S(1)} %get-tuple-element.203, s32[1024]{0:T(1024)S(1)} %get-tuple-element.204, s32[2048]{0:T(1024)S(1)} %get-tuple-element.201, s32[1024]{0:T(1024)S(1)} %get-tuple-element.202), kind=kLoop, calls=%fused_computation.13.clone.1 | loop fusion | flops 29360128 | bytes 16801796 | tf_op jit(solution)/shard_map/while/body/eval_jaxpr/mul | solution.py:30
  1627.0 36.8 %cosine_multiply_fusion.2 = (f32[1024,2048]{1,0:T(8,128)S(1)}, f32[1024,2048]{1,0:T(8,128)}) fusion(s32[]{:T(128)} %bitcast.30, s32[2048]{0:T(1024)S(1)} %get-tuple-element.203, s32[1024]{0:T(1024)S(1)} %get-tuple-element.204, s32[2048]{0:T(1024)S(1)} %get-tuple-element.201, s32[1024]{0:T(1024)S(1)} %get-tuple-element.202), kind=kLoop, calls=%fused_computation.13.clone.1 | loop fusion | flops 29360128 | bytes 16801796 | tf_op jit(solution)/shard_map/while/body/eval_jaxpr/mul | solution.py:30
  1692.6 36.8 %cosine_multiply_fusion.2 = (f32[1024,2048]{1,0:T(8,128)S(1)}, f32[1024,2048]{1,0:T(8,128)}) fusion(s32[]{:T(128)} %bitcast.30, s32[2048]{0:T(1024)S(1)} %get-tuple-element.203, s32[1024]{0:T(1024)S(1)} %get-tuple-element.204, s32[2048]{0:T(1024)S(1)} %get-tuple-element.201, s32[1024]{0:T(1024)S(1)} %get-tuple-element.202), kind=kLoop, calls=%fused_computation.13.clone.1 | loop fusion | flops 29360128 | bytes 16801796 | tf_op jit(solution)/shard_map/while/body/eval_jaxpr/mul | solution.py:30
  1758.3 36.8 %cosine_multiply_fusion.2 = (f32[1024,2048]{1,0:T(8,128)S(1)}, f32[1024,2048]{1,0:T(8,128)}) fusion(s32[]{:T(128)} %bitcast.30, s32[2048]{0:T(1024)S(1)} %get-tuple-element.203, s32[1024]{0:T(1024)S(1)} %get-tuple-element.204, s32[2048]{0:T(1024)S(1)} %get-tuple-element.201, s32[1024]{0:T(1024)S(1)} %get-tuple-element.202), kind=kLoop, calls=%fused_computation.13.clone.1 | loop fusion | flops 29360128 | bytes 16801796 | tf_op jit(solution)/shard_map/while/body/eval_jaxpr/mul | solution.py:30
  1824.0 36.8 %cosine_multiply_fusion.2 = (f32[1024,2048]{1,0:T(8,128)S(1)}, f32[1024,2048]{1,0:T(8,128)}) fusion(s32[]{:T(128)} %bitcast.30, s32[2048]{0:T(1024)S(1)} %get-tuple-element.203, s32[1024]{0:T(1024)S(1)} %get-tuple-element.204, s32[2048]{0:T(1024)S(1)} %get-tuple-element.201, s32[1024]{0:T(1024)S(1)} %get-tuple-element.202), kind=kLoop, calls=%fused_computation.13.clone.1 | loop fusion | flops 29360128 | bytes 16801796 | tf_op jit(solution)/shard_map/while/body/eval_jaxpr/mul | solution.py:30
  1889.6 36.8 %cosine_multiply_fusion.2 = (f32[1024,2048]{1,0:T(8,128)S(1)}, f32[1024,2048]{1,0:T(8,128)}) fusion(s32[]{:T(128)} %bitcast.30, s32[2048]{0:T(1024)S(1)} %get-tuple-element.203, s32[1024]{0:T(1024)S(1)} %get-tuple-element.204, s32[2048]{0:T(1024)S(1)} %get-tuple-element.201, s32[1024]{0:T(1024)S(1)} %get-tuple-element.202), kind=kLoop, calls=%fused_computation.13.clone.1 | loop fusion | flops 29360128 | bytes 16801796 | tf_op jit(solution)/shard_map/while/body/eval_jaxpr/mul | solution.py:30
  1955.3 36.8 %cosine_multiply_fusion.2 = (f32[1024,2048]{1,0:T(8,128)S(1)}, f32[1024,2048]{1,0:T(8,128)}) fusion(s32[]{:T(128)} %bitcast.30, s32[2048]{0:T(1024)S(1)} %get-tuple-element.203, s32[1024]{0:T(1024)S(1)} %get-tuple-element.204, s32[2048]{0:T(1024)S(1)} %get-tuple-element.201, s32[1024]{0:T(1024)S(1)} %get-tuple-element.202), kind=kLoop, calls=%fused_computation.13.clone.1 | loop fusion | flops 29360128 | bytes 16801796 | tf_op jit(solution)/shard_map/while/body/eval_jaxpr/mul | solution.py:30
  2020.9 36.8 %cosine_multiply_fusion.2 = (f32[1024,2048]{1,0:T(8,128)S(1)}, f32[1024,2048]{1,0:T(8,128)}) fusion(s32[]{:T(128)} %bitcast.30, s32[2048]{0:T(1024)S(1)} %get-tuple-element.203, s32[1024]{0:T(1024)S(1)} %get-tuple-element.204, s32[2048]{0:T(1024)S(1)} %get-tuple-element.201, s32[1024]{0:T(1024)S(1)} %get-tuple-element.202), kind=kLoop, calls=%fused_computation.13.clone.1 | loop fusion | flops 29360128 | bytes 16801796 | tf_op jit(solution)/shard_map/while/body/eval_jaxpr/mul | solution.py:30
  2086.6 36.8 %cosine_multiply_fusion.2 = (f32[1024,2048]{1,0:T(8,128)S(1)}, f32[1024,2048]{1,0:T(8,128)}) fusion(s32[]{:T(128)} %bitcast.30, s32[2048]{0:T(1024)S(1)} %get-tuple-element.203, s32[1024]{0:T(1024)S(1)} %get-tuple-element.204, s32[2048]{0:T(1024)S(1)} %get-tuple-element.201, s32[1024]{0:T(1024)S(1)} %get-tuple-element.202), kind=kLoop, calls=%fused_computation.13.clone.1 | loop fusion | flops 29360128 | bytes 16801796 | tf_op jit(solution)/shard_map/while/body/eval_jaxpr/mul | solution.py:30
  2162.8 137.5 %all-to-all-done.1 = f32[24,8,8192]{2,0,1:T(8,128)} async-done(((f32[24,8,8192]{2,0,1:T(8,128)}), f32[24,8,8192]{2,0,1:T(8,128)}, u32[]{:S(2)}, u32[]{:S(2)}) %all-to-all-start.1) | async-done | bytes 6291488 | tf_op jit(solution)/shard_map/all_to_all | solution.py:98
  2338.1 62.2 %fusion.29 = f32[64,128,256]{2,1,0:T(8,128)S(1)} fusion(s32[192,256]{1,0:T(8,128)S(1)} %copy-done.2, f32[192,128,64]{1,2,0:T(8,128)S(1)} %get-tuple-element.114), kind=kOutput, calls=%fused_computation.40 | convolution fusion | flops 4875878400 | bytes 14876672 | tf_op jit(solution)/shard_map/kcd,cbk->dbk/dot_general | solution.py:61
  2400.3 62.4 %fusion.27 = f32[64,128,256]{2,1,0:T(8,128)S(1)} fusion(s32[192,256]{1,0:T(8,128)S(1)} %copy-done.2, f32[192,128,64]{1,2,0:T(8,128)S(1)} %copy-done), kind=kOutput, calls=%fused_computation.39 | convolution fusion | flops 4875878400 | bytes 14876672 | tf_op jit(solution)/shard_map/kcd,cbk->dbk/dot_general | solution.py:63
  2462.7 62.6 %subtract_bitcast_fusion = f32[256,128,64]{0,1,2:T(8,128)S(1)} fusion(f32[64,128,256]{2,1,0:T(8,128)S(1)} %fusion.29, s32[192,256]{1,0:T(8,128)S(1)} %copy-done.2, f32[192,128,64]{1,2,0:T(8,128)S(1)} %copy-done), kind=kOutput, calls=%fused_computation.35 | convolution fusion | flops 4877975552 | bytes 23265280 | tf_op jit(solution)/shard_map/kcd,cbk->dbk/dot_general | solution.py:62
  2525.4 63.1 %add_bitcast_fusion = f32[256,128,64]{0,1,2:T(8,128)S(1)} fusion(f32[64,128,256]{2,1,0:T(8,128)S(1)} %fusion.27, s32[192,256]{1,0:T(8,128)S(1)} %copy-done.2, f32[192,128,64]{1,2,0:T(8,128)S(1)} %get-tuple-element.114), kind=kOutput, calls=%fused_computation.34 | convolution fusion | flops 4877975552 | bytes 23265280 | tf_op jit(solution)/shard_map/kcd,cbk->dbk/dot_general | solution.py:64
  2612.9 23.0 fusion.54
  2635.8 70.2 %reduce-scatter.2.cloned.1.call-done = f32[64,128,64]{1,2,0:T(8,128)} async-done(((f32[256,128,64]{1,2,0:T(8,128)}), f32[64,128,64]{1,2,0:T(8,128)}) %reduce-scatter.2.cloned.1.call-update) | async-done | bytes 2097168 | tf_op jit(solution)/shard_map/reduce_scatter | solution.py:100
  (154 shorter events, 460.4 us)
Async XLA Ops:
  6.5 7.4 copy-start.1
  6.5 551.4 %all-to-all-start = ((f32[192,256,128]{2,1,0:T(8,128)}), f32[192,256,128]{2,1,0:T(8,128)}, u32[]{:S(2)}, u32[]{:S(2)}) async-start(f32[192,256,128]{2,1,0:T(8,128)} %param.5), calls=%async_computation | async-start | bytes 50331648 | tf_op jit(solution)/shard_map/all_to_all | solution.py:79
  2157.6 142.7 %all-to-all-start.1 = ((f32[24,8,8192]{2,0,1:T(8,128)}), f32[24,8,8192]{2,0,1:T(8,128)}, u32[]{:S(2)}, u32[]{:S(2)}) async-start(f32[24,8,8192]{2,0,1:T(8,128)} %bitcast.32), calls=%async_computation.1 | async-start | bytes 12582912 | tf_op jit(solution)/shard_map/all_to_all | solution.py:98
  2162.4 543.6 %reduce-scatter.2.cloned.1.call-start = ((), (), s32[]{:S(2)}) async-start(), calls=%async_computation.3 | async-start | bytes 10485760 | tf_op jit(solution)/shard_map/reduce_scatter | solution.py:100
  2328.7 9.4 copy-start.2
  2338.1 62.2 %copy-start = (f32[192,128,64]{1,2,0:T(8,128)S(1)}, f32[192,128,64]{1,2,0:T(8,128)}, u32[]{:S(2)}) copy-start(f32[192,128,64]{1,2,0:T(8,128)} %get-tuple-element.115) | copy-start | bytes 18874372
Sparse Core Ops, SparseCore 0:
  2636.0 70.0 reduce-scatter.1
where the time goes:
time: 2730 us; the launch traced here: 2710 us
  other arithmetic  891 us (33%)
  matrix products  797 us (29%)
  waiting for transfers between devices  752 us (28%)
  local copies, waits for them, and re-layouts  233 us (9%)
    mul x24, other arithmetic, steering(): return (jnp.cos(phases) * factor, jnp.sin(phases) * factor)  883 us
    all_to_all x1, waiting for transfers between devices, body(): lax.all_to_all(voltages, 'feed', split_axis=0, concat_axis=1, tiled=True)  544 us
    dot_general x24, matrix products, beam_power(): products = jnp.dot(weights, voltage, precision=highest)  507 us
    dynamic_update_slice x24, local copies, waits for them, and re-layouts, body(): powers = lax.map(beam_power, (channels, by_channel))  145 us
    all_to_all x1, waiting for transfers between devices, body(): lax.all_to_all(powers, 'feed', split_axis=1, concat_axis=0, tiled=True)  137 us
    reduce_scatter x1, waiting for transfers between devices, body(): lax.psum_scatter(to_series(shifted_rows(spec_real, spec_imag, delays, fra...  70.2 us
    dot_general x1, matrix products, shifted_rows(): jnp.einsum('kcd,cbk->dbk', shift_sin, spec_real, precision=highest)  63.1 us
    dot_general x1, matrix products, shifted_rows(): jnp.einsum('kcd,cbk->dbk', shift_sin, spec_imag, precision=highest)  62.6 us
  transfers between devices with their start and end apart: 3, of which 3 were waited for; matrix products, arithmetic and copies ran while one was open for 0% of the time, Pallas kernels for 0%

commit v1 on v0

v1 whole, which is shorter than its diff:
```python
import functools
import math

import jax
import jax.numpy as jnp
from jax import lax
from jax.experimental import pallas as pl
from jax.experimental.pallas import tpu as pltpu
from jax.sharding import PartitionSpec as P

FEEDS = 2048
CHANNELS = 768
FRAMES = 64
SIDE = 32
BEAMS = 1024
GRID = 64
BINS = FRAMES // 2
LANES = 2 * FRAMES
CHUNK = 8
VMEM_LIMIT = 56 * 1024 * 1024


def high_low(table):
    high = lax.reduce_precision(table, 8, 7)
    return high.astype(jnp.bfloat16), (table - high).astype(jnp.bfloat16)


def halves(values):
    high = values.astype(jnp.bfloat16)
    return high, (values - high.astype(jnp.float32)).astype(jnp.bfloat16)


def steering_tables(channels, offsets):
    lines = jnp.arange(GRID, dtype=jnp.int32)
    residue = jnp.mod(
        offsets[None, :, None] * lines[None, None, :] * (CHANNELS + channels)[:, None, None],
        GRID * CHANNELS,
    )
    phases = residue.astype(jnp.float32) * (2.0 * math.pi / (GRID * CHANNELS))
    high, low = high_low(jnp.concatenate([jnp.cos(phases), jnp.sin(phases)], axis=1))
    return jnp.concatenate([high, high, low], axis=2)


def turned(values):
    swapped = pltpu.roll(values, FRAMES, 1)
    lane = lax.broadcasted_iota(jnp.int32, swapped.shape, 1)
    return jnp.where(lane < FRAMES, swapped, -swapped)


def partial_kernel(cells_ref, *refs, senders, wide):
    volts_ref, first_ref, second_ref = refs[:3]
    mine_ref, theirs_ref, grid_ref, rows_ref = refs[-4:]
    _, kc, feeds_each, _ = volts_ref.shape
    cells = GRID * GRID

    @pl.when(pl.program_id(0) == 0)
    def _():
        grid_ref[...] = jnp.zeros_like(grid_ref)

    for sender in range(senders):

        volts = volts_ref.at[sender].reshape(kc * feeds_each, LANES)

        def place(feed, _, sender=sender, volts=volts):
            cell = cells_ref[sender * feeds_each + feed]
            value = volts[pl.ds(feed, kc, stride=feeds_each), :]
            grid_ref[pl.ds(cell, kc, stride=cells), :] = value
            return 0

        lax.fori_loop(0, feeds_each, place, 0, unroll=8)

    def one_channel(chan, _):
        first = first_ref[chan]
        second = second_ref[chan]

        def column_step(step, _):
            base = chan * cells + step * (wide * GRID)
            block = jnp.concatenate(
                [grid_ref[pl.ds(base + j * GRID, GRID), :] for j in range(wide)], axis=1
            )
            high, low = halves(block)
            sums = jnp.dot(
                first, jnp.concatenate([high, low, high], axis=0), preferred_element_type=jnp.float32
            )
            for j in range(wide):
                part = sums[:, j * LANES : (j + 1) * LANES]
                rows_ref[pl.ds(step * wide + j, SIDE, stride=GRID), :] = part[:SIDE] + turned(part[SIDE:])
            return 0

        lax.fori_loop(0, GRID // wide, column_step, 0, unroll=True)

        def row_step(step, _):
            base = step * (wide * GRID)
            block = jnp.concatenate(
                [rows_ref[pl.ds(base + j * GRID, GRID), :] for j in range(wide)], axis=1
            )
            high, low = halves(block)
            sums = jnp.dot(
                second, jnp.concatenate([high, low, high], axis=0), preferred_element_type=jnp.float32
            )
            for j in range(wide):
                part = sums[:, j * LANES : (j + 1) * LANES]
                beams = part[:SIDE] + turned(part[SIDE:])
                at = chan * (SIDE // 2 * SIDE) + step * wide + j
                mine_ref[pl.ds(at, SIDE // 2, stride=SIDE), :] = beams[: SIDE // 2]
                theirs_ref[pl.ds(at, SIDE // 2, stride=SIDE), :] = beams[SIDE // 2 :]
            return 0

        lax.fori_loop(0, SIDE // wide, row_step, 0, unroll=True)
        return 0

    lax.fori_loop(0, kc, one_channel, 0)


def partial_beams(cells, volts, first, second, kc, after, wide=4):
    senders, cc, feeds_each, _ = volts.shape
    rows = SIDE // 2 * SIDE
    out = jax.ShapeDtypeStruct((cc * rows, LANES), jnp.float32)
    table_spec = pl.BlockSpec((kc,) + first.shape[1:], lambda i, *_: (i, 0, 0))
    out_spec = pl.BlockSpec((kc * rows, LANES), lambda i, *_: (i, 0))
    return pl.pallas_call(
        functools.partial(partial_kernel, senders=senders, wide=wide),
        grid_spec=pltpu.PrefetchScalarGridSpec(
            num_scalar_prefetch=1,
            grid=(cc // kc,),
            in_specs=[
                pl.BlockSpec((senders, kc, feeds_each, LANES), lambda i, *_: (0, i, 0, 0)),
                table_spec,
                table_spec,
            ]
            + [pl.BlockSpec(memory_space=pl.ANY)] * len(after),
            out_specs=[out_spec, out_spec],
            scratch_shapes=[
                pltpu.VMEM((kc * GRID * GRID, LANES), jnp.float32),
                pltpu.VMEM((SIDE * GRID, LANES), jnp.float32),
            ],
        ),
        out_shape=[out, out],
        compiler_params=pltpu.CompilerParams(vmem_limit_bytes=VMEM_LIMIT),
        cost_estimate=pl.CostEstimate(
            flops=cc * 6 * 50_000_000, bytes_accessed=volts.size * 4 + 2 * cc * rows * LANES * 4, transcendentals=0
        ),
        name="partial_beams",
    )(cells, volts, first, second, *after)


def forward_table():
    frames = jnp.arange(FRAMES, dtype=jnp.int32)
    wave = jnp.mod(frames[:, None] * (1 + jnp.arange(BINS, dtype=jnp.int32))[None, :], FRAMES)
    phases = wave.astype(jnp.float32) * (2.0 * math.pi / FRAMES)
    one = jnp.concatenate([jnp.cos(phases), -jnp.sin(phases)], axis=1)
    none = jnp.zeros_like(one)
    both = jnp.concatenate(
        [jnp.concatenate([one, none], axis=1), jnp.concatenate([none, one], axis=1)], axis=0
    )
    high, low = high_low(both)
    return jnp.concatenate([high, high, low], axis=0)


def inverse_table():
    frames = jnp.arange(FRAMES, dtype=jnp.int32)
    bins = 1 + jnp.arange(BINS, dtype=jnp.int32)
    wave = jnp.mod(frames[:, None] * bins[None, :], FRAMES)
    phases = wave.astype(jnp.float32) * (2.0 * math.pi / FRAMES)
    weight = jnp.where(bins < BINS, 2.0, 1.0) * (0.5 / (FRAMES * math.sqrt(CHANNELS) * FEEDS))
    high, low = high_low(jnp.concatenate([jnp.cos(phases) * weight, -jnp.sin(phases) * weight], axis=1))
    return jnp.concatenate([high, high, low], axis=1)


def spectra_kernel(mine_ref, came_ref, table_ref, *refs, kc, split_rows, owners):
    out_refs = refs[-owners:]
    each = out_refs[0].shape[1]
    rows = SIDE // 2 * SIDE
    for chan in range(kc):
        at = pl.ds(chan * rows, rows)
        beams = mine_ref[at, :] + came_ref[at, :]
        square = beams * beams
        power = square + pltpu.roll(square, FRAMES, 1)
        if split_rows:
            left, right = power[: rows // 2], power[rows // 2 :]
        else:
            power = power.reshape(SIDE // 2, 2, SIDE // 2, LANES)
            left = power[:, 0].reshape(rows // 2, LANES)
            right = power[:, 1].reshape(rows // 2, LANES)
        lane = lax.broadcasted_iota(jnp.int32, left.shape, 1)
        high, low = halves(jnp.where(lane < FRAMES, left, right))
        spectra = jnp.dot(
            jnp.concatenate([high, low, high], axis=1), table_ref[...], preferred_element_type=jnp.float32
        )
        for owner in range(owners):
            out_refs[owner][chan] = spectra[owner * each : (owner + 1) * each]


def beam_spectra(mine, came, table, owners, split_rows, kc, after):
    rows = SIDE // 2 * SIDE
    cc = mine.shape[0] // rows
    each = rows // 2 // owners
    block = pl.BlockSpec((kc * rows, LANES), lambda i: (i, 0))
    return pl.pallas_call(
        functools.partial(spectra_kernel, kc=kc, split_rows=split_rows, owners=owners),
        grid=(cc // kc,),
        in_specs=[block, block, pl.BlockSpec(table.shape, lambda i: (0, 0))]
        + [pl.BlockSpec(memory_space=pl.ANY)] * len(after),
        out_specs=[pl.BlockSpec((kc, each, LANES), lambda i: (i, 0, 0))] * owners,
        out_shape=[jax.ShapeDtypeStruct((cc, each, LANES), jnp.float32)] * owners,
        compiler_params=pltpu.CompilerParams(vmem_limit_bytes=VMEM_LIMIT),
        cost_estimate=pl.CostEstimate(
            flops=cc * rows * LANES * LANES * 3, bytes_accessed=mine.size * 12, transcendentals=0
        ),
        name="beam_spectra",
    )(mine, came, table, *after)


def dedisperse_kernel(*refs, chans, each, trials, first, last):
    spectra_ref, cos_ref, sin_ref, inverse_ref = refs[:4]
    held_ref = None if first else refs[4]
    out_ref, bins_ref = refs[-3 if last else -2], refs[-1 if not last else -2]
    total_ref = refs[-1] if last else out_ref
    stack = LANES // each

    def turn_step(step, _):
        block = jnp.transpose(spectra_ref[pl.ds(step * LANES, LANES), :])
        top, bottom = block[:FRAMES], block[FRAMES:]
        lane = lax.broadcasted_iota(jnp.int32, top.shape, 1)
        for e in range(stack):
            left = pltpu.roll(top, (LANES - e * each) % LANES, 1) if e else top
            shift = (each - e * each) % LANES
            right = pltpu.roll(bottom, shift, 1) if shift else bottom
            bins_ref[pl.ds(step * stack + e, FRAMES, stride=chans), :] = jnp.where(lane < each, left, right)
        return 0

    lax.fori_loop(0, chans // stack, turn_step, 0, unroll=4)

    cos_one, sin_one = cos_ref[...], sin_ref[...]

    def bin_step(k, carry):
        cos_k, sin_k = carry
        shift_high, shift_low = halves(jnp.concatenate([cos_k, sin_k], axis=0))
        spec = jnp.concatenate(
            [bins_ref[pl.ds(k * chans, chans), :], bins_ref[pl.ds((BINS + k) * chans, chans), :]], axis=1
        )
        high, low = halves(spec)
        if chans % LANES == 0:
            sums = jnp.dot(
                jnp.concatenate([shift_high, shift_high, shift_low], axis=1),
                jnp.concatenate([high, low, high], axis=0),
                preferred_element_type=jnp.float32,
            )
        else:
            sums = jnp.dot(shift_high, high, preferred_element_type=jnp.float32)
            sums = sums + jnp.dot(shift_high, low, preferred_element_type=jnp.float32)
            sums = sums + jnp.dot(shift_low, high, preferred_element_type=jnp.float32)
        real = sums[:trials, :LANES] - sums[trials:, LANES:]
        imag = sums[:trials, LANES:] + sums[trials:, :LANES]
        at_real, at_imag = pl.ds(k * trials, trials), pl.ds((BINS + k) * trials, trials)
        if held_ref is not None:
            real = real + held_ref[at_real, :]
            imag = imag + held_ref[at_imag, :]
        total_ref[at_real, :] = real
        total_ref[at_imag, :] = imag
        return cos_k * cos_one - sin_k * sin_one, sin_k * cos_one + cos_k * sin_one

    lax.fori_loop(0, BINS, bin_step, (cos_one, sin_one), unroll=4)

    if last:
        wide = 4
        for step in range(trials // wide):
            block = jnp.concatenate(
                [total_ref[pl.ds(step * wide + j, FRAMES, stride=trials), :] for j in range(wide)], axis=1
            )
            high, low = halves(block)
            series = jnp.dot(
                inverse_ref[...], jnp.concatenate([high, low, high], axis=0), preferred_element_type=jnp.float32
            )
            for j in range(wide):
                out_ref[pl.ds((step * wide + j) * FRAMES, FRAMES), :] = series[:, j * LANES : (j + 1) * LANES]


def dedisperse(spectra, cos_one, sin_one, inverse, held, last):
    each = spectra.shape[1]
    trials, chans = cos_one.shape
    rows = trials * FRAMES
    args = [spectra.reshape(chans * each, LANES), cos_one, sin_one, inverse]
    if held is not None:
        args.append(held)
    scratch = [pltpu.VMEM((FRAMES * chans, LANES), jnp.float32)]
    if last:
        scratch.append(pltpu.VMEM((rows, LANES), jnp.float32))
    return pl.pallas_call(
        functools.partial(
            dedisperse_kernel, chans=chans, each=each, trials=trials, first=held is None, last=last
        ),
        in_specs=[pl.BlockSpec(memory_space=pltpu.VMEM)] * len(args),
        out_specs=pl.BlockSpec(memory_space=pltpu.VMEM),
        out_shape=jax.ShapeDtypeStruct((rows, LANES), jnp.float32),
        scratch_shapes=scratch,
        compiler_params=pltpu.CompilerParams(vmem_limit_bytes=VMEM_LIMIT),
        cost_estimate=pl.CostEstimate(
            flops=BINS * 2 * trials * chans * 2 * LANES * 6, bytes_accessed=spectra.size * 8, transcendentals=0
        ),
        name="dedisperse",
    )(*args)


def sizes_of(total, step):
    if total < 2 * step or total % step or step % 2:
        step = math.gcd(total, max(step // 2, 1))
        return [step] * (total // step)
    return [step // 2] + [step] * (total // step - 1) + [step // 2]


def body(voltages, feed_cells, delays):
    band_chans = voltages.shape[0]
    bands, devices = lax.axis_size("band"), lax.axis_size("feed")
    half = devices // 2
    place = lax.axis_index("feed")
    side = place // half
    spot = place % half
    groups = [list(range(half)), list(range(half, devices))]
    partners = spot ^ jnp.arange(half, dtype=jnp.int32)
    opposite = [(j, (j + half) % devices) for j in range(devices)]
    own_chans = band_chans // half
    cells = lax.dynamic_slice_in_dim(feed_cells[:FEEDS], side * (FEEDS // 2), FEEDS // 2)

    beam_rows = SIDE // 2 // half
    split_rows = beam_rows % 2 == 0
    order = jnp.arange(SIDE // 2, dtype=jnp.int32)
    if split_rows:
        order = order.reshape(half, 2, beam_rows // 2)[partners].swapaxes(0, 1).reshape(-1)
    else:
        order = order.reshape(half, beam_rows)[partners].reshape(-1)
    natural = jnp.arange(SIDE, dtype=jnp.int32) - SIDE // 2
    kept = jnp.concatenate([order + side * (SIDE // 2), order + (1 - side) * (SIDE // 2)]) - SIDE // 2

    forward, inverse = forward_table(), inverse_table()
    trials = delays.shape[1] // bands
    shifts = lax.all_to_all(delays, "band", split_axis=1, concat_axis=0, tiled=True)
    shifts = shifts.reshape(bands, band_chans, trials)

    sizes = sizes_of(own_chans, CHUNK)
    starts = [sum(sizes[:i]) for i in range(len(sizes))]
    spans = [slice(a * half, (a + cc) * half) for a, cc in zip(starts, sizes)]
    count = len(sizes)
    volts, mine, theirs, came, spectra, gathered = ([None] * count for _ in range(6))
    held = None

    def swapped(part, step):
        return lax.ppermute(part, "feed", [(j, j ^ step) for j in range(devices)])

    def send_volts(i, *after):
        piece = voltages[spans[i]]
        if after:
            piece = lax.optimization_barrier((piece,) + after)[0]
        volts[i] = lax.all_to_all(
            piece, "feed", split_axis=0, concat_axis=0, axis_index_groups=groups, tiled=True
        ).reshape(half, sizes[i], voltages.shape[1], LANES)

    def form_partial(i, *after):
        cc = sizes[i]
        channels = (
            lax.axis_index("band") * band_chans
            + starts[i] * half
            + spot * cc
            + jnp.arange(cc, dtype=jnp.int32)
        )
        first = steering_tables(channels, natural)
        second = steering_tables(channels, kept)
        mine[i], theirs[i] = partial_beams(cells, volts[i], first, second, math.gcd(cc, 8), after)
        came[i] = lax.ppermute(theirs[i], "feed", opposite)

    def form_spectra(i, *after):
        own = beam_spectra(mine[i], came[i], forward, half, split_rows, math.gcd(sizes[i], 4), after)
        spectra[i] = jnp.concatenate([own[0]] + [swapped(own[step], step) for step in range(1, half)])
        gathered[i] = lax.all_gather(spectra[i], "band")

    def fold(i, held):
        each = gathered[i].shape[-2]
        shift = shifts[:, spans[i]].reshape(bands, half, -1, trials)[:, partners].reshape(-1, trials).T.astype(jnp.float32) * (2.0 * math.pi / FRAMES)
        return dedisperse(
            gathered[i].reshape(-1, each, LANES), jnp.cos(shift), jnp.sin(shift), inverse, held, i == count - 1
        )

    for i in range(min(2, count)):
        send_volts(i)
    for i in range(count + 3):
        if i < count:
            form_partial(i)
        if i + 2 < count:
            send_volts(i + 2, theirs[i])
        if 0 <= i - 3 < count:
            held = fold(i - 3, held)
        if 0 <= i - 1 < count:
            form_spectra(i - 1, *([theirs[i]] if i < count else []), *([held] if held is not None and i - 3 < count - 1 else []))
    each = gathered[0].shape[-2]
    return held.reshape(trials, FRAMES, LANES)[:, :, : 2 * each].swapaxes(1, 2)


def solution(mesh):
    placed = (P("band", "feed", None), P(), P("band", None))
    return jax.shard_map(
        body, mesh=mesh, in_specs=placed, out_specs=P("band", "feed", None), check_vma=False
    )
```

time: 2730 us -> 873 us (0.32)
  other arithmetic: 891 us -> 41.6 us
  matrix products: 797 us -> 0 us
  waiting for transfers between devices: 752 us -> 423 us
  Pallas kernels: 0 us -> 269 us
  local copies, waits for them, and re-layouts: 233 us -> 44.5 us
  starting transfers between devices: 12.3 us -> 71.8 us
    mul x25 -> x4, other arithmetic: 883 us -> 0.93 us  [the longest x1 0.78 us: inverse_table(): jnp.cos(phases) * weight]
    dot_general x30 -> x0, matrix products: 797 us -> none  [the longest x24 507 us: beam_power(): products = jnp.dot(weights, voltage, precision=highest)]
    all_to_all x2 -> x8, waiting for transfers between devices: 681 us -> 80.1 us  [the longest x7 78.7 us: send_volts(): lax.all_to_all(piece, 'feed', split_axis=0, concat_axis=0, axis_index_gro...]
    ppermute x0 -> x28, waiting for transfers between devices: none -> 339 us  [the longest x7 264 us: form_partial(): came[i] = lax.ppermute(theirs[i], 'feed', opposite)]
    pallas_call x0 -> x21, Pallas kernels: none -> 269 us  [the longest x7 159 us: partial_beams(): pl.pallas_call(functools.partial(partial_kernel, senders=senders, wide=wi...]
    dynamic_update_slice x24 -> x0, local copies, waits for them, and re-layouts: 145 us -> none  [body(): powers = lax.map(beam_power, (channels, by_channel))]
    reduce_scatter x1 -> x0, waiting for transfers between devices: 70.2 us -> none  [body(): lax.psum_scatter(to_series(shifted_rows(spec_real, spec_imag, delays, fra...]
    ppermute x0 -> x28, starting transfers between devices: none -> 33 us  [the longest x21 27.6 us: swapped(): return lax.ppermute(part, 'feed', [(j, j ^ step) for j in range(devices)])]
  transfers between devices with their start and end apart: 3 -> 43, of which waited for: 3 -> 32; matrix products, arithmetic and copies ran while one was open for 0% -> 9% of each run, Pallas kernels for 0% -> 30%
where the time goes in v1:
time: 873 us; the launch traced here: 864 us
  waiting for transfers between devices  423 us (48%)
  Pallas kernels  269 us (31%)
  starting transfers between devices  71.8 us (8%)
  local copies, waits for them, and re-layouts  44.5 us (5%)
  other arithmetic  41.6 us (5%)
  between operations  14.5 us (2%)
    ppermute x7, waiting for transfers between devices, form_partial(): came[i] = lax.ppermute(theirs[i], 'feed', opposite)  264 us
    pallas_call x7, Pallas kernels, partial_beams(): pl.pallas_call(functools.partial(partial_kernel, senders=senders, wide=wi...  159 us
    pallas_call x7, Pallas kernels, dedisperse(): pl.pallas_call(functools.partial(dedisperse_kernel, chans=chans, each=eac...  86.6 us
    all_to_all x7, waiting for transfers between devices, send_volts(): lax.all_to_all(piece, 'feed', split_axis=0, concat_axis=0, axis_index_gro...  78.7 us
    ppermute x21, waiting for transfers between devices, swapped(): return lax.ppermute(part, 'feed', [(j, j ^ step) for j in range(devices)])  74.9 us
    all_to_all x7, starting transfers between devices, send_volts(): lax.all_to_all(piece, 'feed', split_axis=0, concat_axis=0, axis_index_gro...  33.6 us
    ppermute x21, starting transfers between devices, swapped(): return lax.ppermute(part, 'feed', [(j, j ^ step) for j in range(devices)])  27.6 us
    pallas_call x7, Pallas kernels, beam_spectra(): pl.pallas_call(functools.partial(spectra_kernel, kc=kc, split_rows=split_...  22.7 us
  transfers between devices with their start and end apart: 43, of which 32 were waited for; matrix products, arithmetic and copies ran while one was open for 9% of the time, Pallas kernels for 30%

profile of v1, /device:TPU:0, one launch (start us, length us, event | category | flops | bytes accessed | tf_op | source)
XLA Modules:
  0.0 863.8 jit_solution(6422618291704483456)
XLA Ops:
  8.3 4.2 all-to-all-start.7
  12.5 4.7 fusion.124
  18.5 4.4 all-to-all-start
  23.0 14.9 %fusion.123 = (f32[32,256,128]{2,1,0:T(8,128)}, f32[32,256,128]{2,1,0:T(8,128)}, f32[32,256,128]{2,1,0:T(8,128)}, f32[32,256,128]{2,1,0:T(8,128)}, f32[32,256,128]{2,1,0:T(8,128)}) fusion(f32[192,256,128]{2,1,0:T(8,128)} %param.3), kind=kLoop, calls=%fused_computation.275 | loop fusion | bytes 41943040 | tf_op jit(solution)/shard_map/slice | solution.py:351
  37.8 9.8 %all-to-all-done = f32[16,256,128]{2,1,0:T(8,128)S(1)} async-done(((f32[16,256,128]{2,1,0:T(8,128)}), f32[16,256,128]{2,1,0:T(8,128)S(1)}, u32[]{:S(2)}, u32[]{:S(2)}) %all-to-all-start) | async-done | bytes 2097184 | tf_op jit(solution)/shard_map/all_to_all | solution.py:354
  49.0 4.8 all-to-all-start.4
  58.9 14.5 %partial_beams.7 = (f32[2048,128]{1,0:T(8,128)}, f32[2048,128]{1,0:T(8,128)}) custom-call(s32[1024]{0:T(1024)} %dynamic_slice.3.cells_ref, f32[4,4,256,128]{3,2,1,0:T(8,128)} %bitcast.96, bf16[4,64,192]{2,1,0:T(8,128)(2,1)} %pad_maximum_fusion.28.refs_1_, bf16[4,64,192]{2,1,0:T(8,128)(2,1)} %pad_maximum_fusion.30.refs_2_), custom_call_target="tpu_custom_call" | custom-call | flops 1200000000 | bytes 4194304 | tf_op jit(solution)/shard_map/partial_beams/pallas_call | solution.py:121
  73.4 28.0 %all-to-all-done.4 = f32[32,256,128]{2,1,0:T(8,128)} async-done(((f32[32,256,128]{2,1,0:T(8,128)}), f32[32,256,128]{2,1,0:T(8,128)}, u32[]{:S(2)}, u32[]{:S(2)}) %all-to-all-start.4) | async-done | bytes 4194336 | tf_op jit(solution)/shard_map/all_to_all | solution.py:354
  101.4 4.9 all-to-all-start.1
  110.6 6.3 fusion.41
  118.8 25.9 %partial_beams.11 = (f32[4096,128]{1,0:T(8,128)}, f32[4096,128]{1,0:T(8,128)}) custom-call(s32[1024]{0:T(1024)} %dynamic_slice.3.cells_ref, f32[4,8,256,128]{3,2,1,0:T(8,128)} %bitcast.7.refs_0_, bf16[8,64,192]{2,1,0:T(8,128)(2,1)} %pad_maximum_fusion.16.refs_1_, bf16[8,64,192]{2,1,0:T(8,128)(2,1)} %pad_maximum_fusion.18.refs_2_), custom_call_target="tpu_custom_call" | custom-call | flops 2400000000 | bytes 8388608 | tf_op jit(solution)/shard_map/partial_beams/pallas_call | solution.py:121
  144.7 28.4 %collective-permute-done.3.came_ref = f32[2048,128]{1,0:T(8,128)S(1)} collective-permute-done((f32[2048,128]{1,0:T(8,128)S(1)}, f32[2048,128]{1,0:T(8,128)S(1)}, u32[]{:S(2)}, u32[]{:S(2)}) %collective-permute-start.3) | collective-permute-done | bytes 1048608 | tf_op jit(solution)/shard_map/ppermute | solution.py:369
  178.6 4.6 collective-permute-start.5
  191.1 4.8 all-to-all-start.5
  199.4 26.0 %partial_beams.8 = (f32[4096,128]{1,0:T(8,128)}, f32[4096,128]{1,0:T(8,128)}) custom-call(s32[1024]{0:T(1024)} %dynamic_slice.3.cells_ref, f32[4,8,256,128]{3,2,1,0:T(8,128)} %bitcast.4.refs_0_, bf16[8,64,192]{2,1,0:T(8,128)(2,1)} %pad_maximum_fusion.8.refs_1_, bf16[8,64,192]{2,1,0:T(8,128)(2,1)} %pad_maximum_fusion.10.refs_2_), custom_call_target="tpu_custom_call" | custom-call | flops 2400000000 | bytes 8388608 | tf_op jit(solution)/shard_map/partial_beams/pallas_call | solution.py:121
  225.5 56.3 %collective-permute-done.10.came_ref = f32[4096,128]{1,0:T(8,128)S(1)} collective-permute-done((f32[4096,128]{1,0:T(8,128)}, f32[4096,128]{1,0:T(8,128)S(1)}, u32[]{:S(2)}, u32[]{:S(2)}) %collective-permute-start.10) | collective-permute-done | bytes 2097184 | tf_op jit(solution)/shard_map/ppermute | solution.py:369
  290.0 5.0 collective-permute-done.11
  296.4 5.3 collective-permute-done.13
  310.4 4.9 all-to-all-start.2
  316.9 8.9 %dedisperse.7.refs_1_.refs_4_ = f32[4096,128]{1,0:T(8,128)} custom-call(f32[4096,128]{1,0:T(8,128)} %bitcast.97, f32[64,64]{1,0:T(8,128)} %bitcast.126, f32[64,64]{1,0:T(8,128)} %bitcast.125, bf16[64,192]{1,0:T(8,128)(2,1)} %pad_maximum_fusion.37.refs_3_), custom_call_target="tpu_custom_call" | custom-call | flops 402653184 | bytes 4194304 | tf_op jit(solution)/shard_map/dedisperse/pallas_call | solution.py:289
  325.8 26.0 %partial_beams.12 = (f32[4096,128]{1,0:T(8,128)}, f32[4096,128]{1,0:T(8,128)}) custom-call(s32[1024]{0:T(1024)} %dynamic_slice.3.cells_ref, f32[4,8,256,128]{3,2,1,0:T(8,128)} %bitcast.8.refs_0_, bf16[8,64,192]{2,1,0:T(8,128)(2,1)} %pad_maximum_fusion.20.refs_1_, bf16[8,64,192]{2,1,0:T(8,128)(2,1)} %pad_maximum_fusion.22.refs_2_), custom_call_target="tpu_custom_call" | custom-call | flops 2400000000 | bytes 8388608 | tf_op jit(solution)/shard_map/partial_beams/pallas_call | solution.py:121
  351.8 44.4 %collective-permute-done.2.came_ref = f32[4096,128]{1,0:T(8,128)} collective-permute-done((f32[4096,128]{1,0:T(8,128)S(1)}, f32[4096,128]{1,0:T(8,128)}, u32[]{:S(2)}, u32[]{:S(2)}) %collective-permute-start.2) | collective-permute-done | bytes 2097184 | tf_op jit(solution)/shard_map/ppermute | solution.py:369
  403.2 4.8 collective-permute-done.7
  408.0 6.3 collective-permute-done.8
  414.4 4.3 collective-permute-done.9
  425.2 5.2 all-to-all-start.6
  430.6 26.0 %partial_beams.9 = (f32[4096,128]{1,0:T(8,128)}, f32[4096,128]{1,0:T(8,128)}) custom-call(s32[1024]{0:T(1024)} %dynamic_slice.3.cells_ref, f32[4,8,256,128]{3,2,1,0:T(8,128)} %bitcast.5.refs_0_, bf16[8,64,192]{2,1,0:T(8,128)(2,1)} %pad_maximum_fusion.12.refs_1_, bf16[8,64,192]{2,1,0:T(8,128)(2,1)} %pad_maximum_fusion.14.refs_2_), custom_call_target="tpu_custom_call" | custom-call | flops 2400000000 | bytes 8388608 | tf_op jit(solution)/shard_map/partial_beams/pallas_call | solution.py:121
  456.6 13.1 %dedisperse.8.refs_4_.refs_1_ = f32[4096,128]{1,0:T(8,128)} custom-call(f32[8192,128]{1,0:T(8,128)} %bitcast.90, f32[64,128]{1,0:T(8,128)} %bitcast.114, f32[64,128]{1,0:T(8,128)} %bitcast.113, bf16[64,192]{1,0:T(8,128)(2,1)} %pad_maximum_fusion.37.refs_3_, f32[4096,128]{1,0:T(8,128)} %dedisperse.7.refs_1_.refs_4_), custom_call_target="tpu_custom_call" | custom-call | flops 805306368 | bytes 8388608 | tf_op jit(solution)/shard_map/dedisperse/pallas_call | solution.py:289
  469.7 41.9 %collective-permute-done.17.came_ref = f32[4096,128]{1,0:T(8,128)} collective-permute-done((f32[4096,128]{1,0:T(8,128)S(1)}, f32[4096,128]{1,0:T(8,128)}, u32[]{:S(2)}, u32[]{:S(2)}) %collective-permute-start.17) | collective-permute-done | bytes 2097184 | tf_op jit(solution)/shard_map/ppermute | solution.py:369
  518.5 4.9 collective-permute-done.18
  523.4 6.1 collective-permute-done.19
  539.1 26.5 %partial_beams.13 = (f32[4096,128]{1,0:T(8,128)}, f32[4096,128]{1,0:T(8,128)}) custom-call(s32[1024]{0:T(1024)} %dynamic_slice.3.cells_ref, f32[4,8,256,128]{3,2,1,0:T(8,128)} %bitcast.9.refs_0_, bf16[8,64,192]{2,1,0:T(8,128)(2,1)} %pad_maximum_fusion.24.refs_1_, bf16[8,64,192]{2,1,0:T(8,128)(2,1)} %pad_maximum_fusion.26.refs_2_), custom_call_target="tpu_custom_call" | custom-call | flops 2400000000 | bytes 8388608 | tf_op jit(solution)/shard_map/partial_beams/pallas_call | solution.py:121
  565.6 13.2 %dedisperse.9.refs_1_.refs_4_ = f32[4096,128]{1,0:T(8,128)} custom-call(f32[8192,128]{1,0:T(8,128)} %bitcast.91, f32[64,128]{1,0:T(8,128)} %bitcast.118, f32[64,128]{1,0:T(8,128)} %bitcast.116, bf16[64,192]{1,0:T(8,128)(2,1)} %pad_maximum_fusion.37.refs_3_, f32[4096,128]{1,0:T(8,128)} %dedisperse.8.refs_4_.refs_1_), custom_call_target="tpu_custom_call" | custom-call | flops 805306368 | bytes 8388608 | tf_op jit(solution)/shard_map/dedisperse/pallas_call | solution.py:289
  578.8 46.2 %collective-permute-done.1.came_ref = f32[4096,128]{1,0:T(8,128)} collective-permute-done((f32[4096,128]{1,0:T(8,128)S(1)}, f32[4096,128]{1,0:T(8,128)}, u32[]{:S(2)}, u32[]{:S(2)}) %collective-permute-start.1) | collective-permute-done | bytes 2097184 | tf_op jit(solution)/shard_map/ppermute | solution.py:369
  631.9 5.0 collective-permute-done.14
  638.5 5.1 collective-permute-done.16
  645.8 4.6 all-to-all-start.3
  655.8 41.0 %all-to-all-done.3 = f32[16,256,128]{2,1,0:T(8,128)} async-done(((f32[16,256,128]{2,1,0:T(8,128)}), f32[16,256,128]{2,1,0:T(8,128)}, u32[]{:S(2)}, u32[]{:S(2)}) %all-to-all-start.3) | async-done | bytes 2097184 | tf_op jit(solution)/shard_map/all_to_all | solution.py:354
  696.7 14.4 %partial_beams.10 = (f32[2048,128]{1,0:T(8,128)}, f32[2048,128]{1,0:T(8,128)}) custom-call(s32[1024]{0:T(1024)} %dynamic_slice.3.cells_ref, f32[4,4,256,128]{3,2,1,0:T(8,128)} %bitcast.6.refs_0_, bf16[4,64,192]{2,1,0:T(8,128)(2,1)} %pad_maximum_fusion.32.refs_1_, bf16[4,64,192]{2,1,0:T(8,128)(2,1)} %pad_maximum_fusion.34.refs_2_), custom_call_target="tpu_custom_call" | custom-call | flops 1200000000 | bytes 4194304 | tf_op jit(solution)/shard_map/partial_beams/pallas_call | solution.py:121
  711.1 13.1 %dedisperse.10.refs_4_.refs_1_ = f32[4096,128]{1,0:T(8,128)} custom-call(f32[8192,128]{1,0:T(8,128)} %bitcast.92, f32[64,128]{1,0:T(8,128)} %bitcast.117, f32[64,128]{1,0:T(8,128)} %bitcast.115, bf16[64,192]{1,0:T(8,128)(2,1)} %pad_maximum_fusion.37.refs_3_, f32[4096,128]{1,0:T(8,128)} %dedisperse.9.refs_1_.refs_4_), custom_call_target="tpu_custom_call" | custom-call | flops 805306368 | bytes 8388608 | tf_op jit(solution)/shard_map/dedisperse/pallas_call | solution.py:289
  724.2 19.1 %collective-permute-done.24.came_ref = f32[4096,128]{1,0:T(8,128)S(1)} collective-permute-done((f32[4096,128]{1,0:T(8,128)}, f32[4096,128]{1,0:T(8,128)S(1)}, u32[]{:S(2)}, u32[]{:S(2)}) %collective-permute-start.24) | collective-permute-done | bytes 2097184 | tf_op jit(solution)/shard_map/ppermute | solution.py:369
  744.6 3.5 beam_spectra.13
  751.6 5.4 collective-permute-done.25
  767.1 13.6 %dedisperse.11.refs_0_.refs_4_ = f32[4096,128]{1,0:T(8,128)} custom-call(f32[8192,128]{1,0:T(8,128)} %bitcast.93, f32[64,128]{1,0:T(8,128)} %bitcast.121, f32[64,128]{1,0:T(8,128)} %bitcast.119, bf16[64,192]{1,0:T(8,128)(2,1)} %pad_maximum_fusion.37.refs_3_, f32[4096,128]{1,0:T(8,128)} %dedisperse.10.refs_4_.refs_1_), custom_call_target="tpu_custom_call" | custom-call | flops 805306368 | bytes 8388608 | tf_op jit(solution)/shard_map/dedisperse/pallas_call | solution.py:289
  780.6 27.7 %collective-permute-done.came_ref = f32[2048,128]{1,0:T(8,128)S(1)} collective-permute-done((f32[2048,128]{1,0:T(8,128)S(1)}, f32[2048,128]{1,0:T(8,128)S(1)}, u32[]{:S(2)}, u32[]{:S(2)}) %collective-permute-start) | collective-permute-done | bytes 1048608 | tf_op jit(solution)/shard_map/ppermute | solution.py:369
  828.1 13.7 %dedisperse.12.refs_4_ = f32[4096,128]{1,0:T(8,128)} custom-call(f32[8192,128]{1,0:T(8,128)} %bitcast.94, f32[64,128]{1,0:T(8,128)} %bitcast.122, f32[64,128]{1,0:T(8,128)} %bitcast.120, bf16[64,192]{1,0:T(8,128)(2,1)} %pad_maximum_fusion.37.refs_3_, f32[4096,128]{1,0:T(8,128)} %dedisperse.11.refs_0_.refs_4_), custom_call_target="tpu_custom_call" | custom-call | flops 805306368 | bytes 8388608 | tf_op jit(solution)/shard_map/dedisperse/pallas_call | solution.py:289
  841.8 3.6 all-gather.25.cloned.1.call-done
  845.5 11.1 %dedisperse.13 = f32[4096,128]{1,0:T(8,128)} custom-call(f32[4096,128]{1,0:T(8,128)} %bitcast.95, f32[64,64]{1,0:T(8,128)} %bitcast.124, f32[64,64]{1,0:T(8,128)} %bitcast.123, bf16[64,192]{1,0:T(8,128)(2,1)} %pad_maximum_fusion.37.refs_3_, f32[4096,128]{1,0:T(8,128)} %dedisperse.12.refs_4_), custom_call_target="tpu_custom_call" | custom-call | flops 402653184 | bytes 4194304 | tf_op jit(solution)/shard_map/dedisperse/pallas_call | solution.py:289
  (211 shorter events, 132.9 us)
Async XLA Ops:
  8.3 10.2 %all-to-all-start.7 = ((s32[192,4,64]{0,2,1:T(8,128)}), s32[192,4,64]{0,2,1:T(8,128)S(1)}, u32[]{:S(2)}, u32[]{:S(2)}) async-start(s32[192,4,64]{0,2,1:T(8,128)} %bitcast.11), calls=%async_computation.7 | async-start | bytes 524288 | tf_op jit(solution)/shard_map/all_to_all | solution.py:337
  18.5 29.1 %all-to-all-start = ((f32[16,256,128]{2,1,0:T(8,128)}), f32[16,256,128]{2,1,0:T(8,128)S(1)}, u32[]{:S(2)}, u32[]{:S(2)}) async-start(f32[16,256,128]{2,1,0:T(8,128)} %get-tuple-element.104), calls=%async_computation | async-start | bytes 4194304 | tf_op jit(solution)/shard_map/all_to_all | solution.py:354
  49.0 52.4 %all-to-all-start.4 = ((f32[32,256,128]{2,1,0:T(8,128)}), f32[32,256,128]{2,1,0:T(8,128)}, u32[]{:S(2)}, u32[]{:S(2)}) async-start(f32[32,256,128]{2,1,0:T(8,128)} %get-tuple-element.99), calls=%async_computation.4 | async-start | bytes 8388608 | tf_op jit(solution)/shard_map/all_to_all | solution.py:354
  73.4 33.9 %copy-start.14 = (f32[2048,128]{1,0:T(8,128)S(1)}, f32[2048,128]{1,0:T(8,128)}, u32[]{:S(2)}) copy-start(f32[2048,128]{1,0:T(8,128)} %get-tuple-element.52) | copy-start | bytes 3145732
  101.4 89.8 %all-to-all-start.1 = ((f32[32,256,128]{2,1,0:T(8,128)}), f32[32,256,128]{2,1,0:T(8,128)}, u32[]{:S(2)}, u32[]{:S(2)}) async-start(f32[32,256,128]{2,1,0:T(8,128)} %get-tuple-element.53), calls=%async_computation.1 | async-start | bytes 8388608 | tf_op jit(solution)/shard_map/all_to_all | solution.py:354
  106.2 210.7 %all-gather.15.cloned.1.call-start = ((), (), s32[]{:S(2)}) async-start(), calls=%async_computation.8 | async-start | bytes 2621440 | tf_op jit(solution)/shard_map/all_gather | solution.py:374
  107.3 65.9 %collective-permute-start.3 = (f32[2048,128]{1,0:T(8,128)S(1)}, f32[2048,128]{1,0:T(8,128)S(1)}, u32[]{:S(2)}, u32[]{:S(2)}) collective-permute-start(f32[2048,128]{1,0:T(8,128)S(1)} %copy-done.14), channel_id=1, source_target_pairs={{0,4},{1,5},{2,6},{3,7},{4,0},{5,1},{6,2},{7,3},{8,12},{9,13},{10,... | collective-permute-start | bytes 3145736 | tf_op jit(solution)/shard_map/ppermute | solution.py:369
  176.9 6.5 collective-permute-start.4
  178.6 8.0 collective-permute-start.5
  183.2 6.1 collective-permute-start.6
  191.0 90.7 %collective-permute-start.10 = (f32[4096,128]{1,0:T(8,128)}, f32[4096,128]{1,0:T(8,128)S(1)}, u32[]{:S(2)}, u32[]{:S(2)}) collective-permute-start(f32[4096,128]{1,0:T(8,128)} %get-tuple-element.61.refs_0_), channel_id=1, source_target_pairs={{0,4},{1,5},{2,6},{3,7},{4,0},{5,1},{6,2},{7,3},{8,12},{9,13},{10,... | collective-permute-start | bytes 6291464 | tf_op jit(solution)/shard_map/ppermute | solution.py:369
  191.1 119.2 %all-to-all-start.5 = ((f32[32,256,128]{2,1,0:T(8,128)}), f32[32,256,128]{2,1,0:T(8,128)}, u32[]{:S(2)}, u32[]{:S(2)}) async-start(f32[32,256,128]{2,1,0:T(8,128)} %get-tuple-element.62), calls=%async_computation.5 | async-start | bytes 8388608 | tf_op jit(solution)/shard_map/all_to_all | solution.py:354
  196.0 260.6 %all-gather.19.cloned.1.call-start = ((), (), s32[]{:S(2)}) async-start(), calls=%async_computation.10 | async-start | bytes 5242880 | tf_op jit(solution)/shard_map/all_gather | solution.py:374
  286.5 17.3 %copy-start = (f32[4096,128]{1,0:T(8,128)S(1)}, f32[4096,128]{1,0:T(8,128)}, u32[]{:S(2)}) copy-start(f32[4096,128]{1,0:T(8,128)} %get-tuple-element.54.refs_0_) | copy-start | bytes 6291460
  286.5 8.6 collective-permute-start.11
  287.0 9.4 %collective-permute-start.12 = (f32[8,64,128]{2,1,0:T(8,128)}, f32[8,64,128]{2,1,0:T(8,128)S(1)}, u32[]{:S(2)}, u32[]{:S(2)}) collective-permute-start(f32[8,64,128]{2,1,0:T(8,128)} %get-tuple-element.79), channel_id=1, source_target_pairs={{0,2},{1,3},{2,0},{3,1},{4,6},{5,7},{6,4},{7,5},{8,10},{9,11},{10,... | collective-permute-start | bytes 786440 | tf_op jit(solution)/shard_map/ppermute | solution.py:348
  287.0 14.7 %collective-permute-start.13 = (f32[8,64,128]{2,1,0:T(8,128)}, f32[8,64,128]{2,1,0:T(8,128)S(1)}, u32[]{:S(2)}, u32[]{:S(2)}) collective-permute-start(f32[8,64,128]{2,1,0:T(8,128)} %get-tuple-element.80), channel_id=1, source_target_pairs={{0,3},{1,2},{2,1},{3,0},{4,7},{5,6},{6,5},{7,4},{8,11},{9,10},{10,... | collective-permute-start | bytes 786440 | tf_op jit(solution)/shard_map/ppermute | solution.py:348
  303.8 92.4 %collective-permute-start.2 = (f32[4096,128]{1,0:T(8,128)S(1)}, f32[4096,128]{1,0:T(8,128)}, u32[]{:S(2)}, u32[]{:S(2)}) collective-permute-start(f32[4096,128]{1,0:T(8,128)S(1)} %copy-done), channel_id=1, source_target_pairs={{0,4},{1,5},{2,6},{3,7},{4,0},{5,1},{6,2},{7,3},{8,12},{9,13},{10,... | collective-permute-start | bytes 6291464 | tf_op jit(solution)/shard_map/ppermute | solution.py:369
  310.4 114.8 %all-to-all-start.2 = ((f32[32,256,128]{2,1,0:T(8,128)}), f32[32,256,128]{2,1,0:T(8,128)}, u32[]{:S(2)}, u32[]{:S(2)}) async-start(f32[32,256,128]{2,1,0:T(8,128)} %get-tuple-element.55), calls=%async_computation.2 | async-start | bytes 8388608 | tf_op jit(solution)/shard_map/all_to_all | solution.py:354
  315.2 250.4 %all-gather.17.cloned.1.call-start = ((), (), s32[]{:S(2)}) async-start(), calls=%async_computation.9 | async-start | bytes 5242880 | tf_op jit(solution)/shard_map/all_gather | solution.py:374
  399.6 21.1 %copy-start.4 = (f32[4096,128]{1,0:T(8,128)S(1)}, f32[4096,128]{1,0:T(8,128)}, u32[]{:S(2)}) copy-start(f32[4096,128]{1,0:T(8,128)} %get-tuple-element.63.refs_0_) | copy-start | bytes 6291460
  399.6 8.4 collective-permute-start.7
  400.0 14.4 %collective-permute-start.8 = (f32[8,64,128]{2,1,0:T(8,128)}, f32[8,64,128]{2,1,0:T(8,128)S(1)}, u32[]{:S(2)}, u32[]{:S(2)}) collective-permute-start(f32[8,64,128]{2,1,0:T(8,128)} %get-tuple-element.74), channel_id=1, source_target_pairs={{0,2},{1,3},{2,0},{3,1},{4,6},{5,7},{6,4},{7,5},{8,10},{9,11},{10,... | collective-permute-start | bytes 786440 | tf_op jit(solution)/shard_map/ppermute | solution.py:348
  400.0 18.7 %collective-permute-start.9 = (f32[8,64,128]{2,1,0:T(8,128)}, f32[8,64,128]{2,1,0:T(8,128)S(1)}, u32[]{:S(2)}, u32[]{:S(2)}) collective-permute-start(f32[8,64,128]{2,1,0:T(8,128)} %get-tuple-element.75), channel_id=1, source_target_pairs={{0,3},{1,2},{2,1},{3,0},{4,7},{5,6},{6,5},{7,4},{8,11},{9,10},{10,... | collective-permute-start | bytes 786440 | tf_op jit(solution)/shard_map/ppermute | solution.py:348
  420.7 90.8 %collective-permute-start.17 = (f32[4096,128]{1,0:T(8,128)S(1)}, f32[4096,128]{1,0:T(8,128)}, u32[]{:S(2)}, u32[]{:S(2)}) collective-permute-start(f32[4096,128]{1,0:T(8,128)S(1)} %copy-done.4), channel_id=1, source_target_pairs={{0,4},{1,5},{2,6},{3,7},{4,0},{5,1},{6,2},{7,3},{8,12},{9,13},{10,... | collective-permute-start | bytes 6291464 | tf_op jit(solution)/shard_map/ppermute | solution.py:369
  425.2 113.9 %all-to-all-start.6 = ((f32[32,256,128]{2,1,0:T(8,128)}), f32[32,256,128]{2,1,0:T(8,128)}, u32[]{:S(2)}, u32[]{:S(2)}) async-start(f32[32,256,128]{2,1,0:T(8,128)} %get-tuple-element.64), calls=%async_computation.6 | async-start | bytes 8388608 | tf_op jit(solution)/shard_map/all_to_all | solution.py:354
  430.3 280.8 %all-gather.23.cloned.1.call-start = ((), (), s32[]{:S(2)}) async-start(), calls=%async_computation.12 | async-start | bytes 5242880 | tf_op jit(solution)/shard_map/all_gather | solution.py:374
  515.0 19.9 %copy-start.5 = (f32[4096,128]{1,0:T(8,128)S(1)}, f32[4096,128]{1,0:T(8,128)}, u32[]{:S(2)}) copy-start(f32[4096,128]{1,0:T(8,128)} %get-tuple-element.56.refs_0_) | copy-start | bytes 6291460
  515.0 20.0 %copy-start.9 = (f32[8,32,64]{2,1,0:T(8,128)S(1)}, f32[8,32,64]{2,1,0:T(8,128)}, u32[]{:S(2)}) copy-start(f32[8,32,64]{2,1,0:T(8,128)} %get-tuple-element.218) | copy-start | bytes 196612
  515.0 8.4 collective-permute-start.18
  515.4 14.1 %collective-permute-start.19 = (f32[8,64,128]{2,1,0:T(8,128)}, f32[8,64,128]{2,1,0:T(8,128)S(1)}, u32[]{:S(2)}, u32[]{:S(2)}) collective-permute-start(f32[8,64,128]{2,1,0:T(8,128)} %get-tuple-element.88), channel_id=1, source_target_pairs={{0,2},{1,3},{2,0},{3,1},{4,6},{5,7},{6,4},{7,5},{8,10},{9,11},{10,... | collective-permute-start | bytes 786440 | tf_op jit(solution)/shard_map/ppermute | solution.py:348
  515.4 17.3 %collective-permute-start.20 = (f32[8,64,128]{2,1,0:T(8,128)}, f32[8,64,128]{2,1,0:T(8,128)S(1)}, u32[]{:S(2)}, u32[]{:S(2)}) collective-permute-start(f32[8,64,128]{2,1,0:T(8,128)} %get-tuple-element.89), channel_id=1, source_target_pairs={{0,3},{1,2},{2,1},{3,0},{4,7},{5,6},{6,5},{7,4},{8,11},{9,10},{10,... | collective-permute-start | bytes 786440 | tf_op jit(solution)/shard_map/ppermute | solution.py:348
  534.8 232.3 %all-gather.21.cloned.1.call-start = ((), (), s32[]{:S(2)}) async-start(), calls=%async_computation.11 | async-start | bytes 5242880 | tf_op jit(solution)/shard_map/all_gather | solution.py:374
  534.8 90.2 %collective-permute-start.1 = (f32[4096,128]{1,0:T(8,128)S(1)}, f32[4096,128]{1,0:T(8,128)}, u32[]{:S(2)}, u32[]{:S(2)}) collective-permute-start(f32[4096,128]{1,0:T(8,128)S(1)} %copy-done.5), channel_id=1, source_target_pairs={{0,4},{1,5},{2,6},{3,7},{4,0},{5,1},{6,2},{7,3},{8,12},{9,13},{10,... | collective-permute-start | bytes 6291464 | tf_op jit(solution)/shard_map/ppermute | solution.py:369
  628.4 8.5 collective-permute-start.14
  629.1 9.4 %collective-permute-start.15 = (f32[8,64,128]{2,1,0:T(8,128)}, f32[8,64,128]{2,1,0:T(8,128)S(1)}, u32[]{:S(2)}, u32[]{:S(2)}) collective-permute-start(f32[8,64,128]{2,1,0:T(8,128)} %get-tuple-element.83), channel_id=1, source_target_pairs={{0,2},{1,3},{2,0},{3,1},{4,6},{5,7},{6,4},{7,5},{8,10},{9,11},{10,... | collective-permute-start | bytes 786440 | tf_op jit(solution)/shard_map/ppermute | solution.py:348
  629.1 14.6 %collective-permute-start.16 = (f32[8,64,128]{2,1,0:T(8,128)}, f32[8,64,128]{2,1,0:T(8,128)S(1)}, u32[]{:S(2)}, u32[]{:S(2)}) collective-permute-start(f32[8,64,128]{2,1,0:T(8,128)} %get-tuple-element.84), channel_id=1, source_target_pairs={{0,3},{1,2},{2,1},{3,0},{4,7},{5,6},{6,5},{7,4},{8,11},{9,10},{10,... | collective-permute-start | bytes 786440 | tf_op jit(solution)/shard_map/ppermute | solution.py:348
  645.8 50.9 %all-to-all-start.3 = ((f32[16,256,128]{2,1,0:T(8,128)}), f32[16,256,128]{2,1,0:T(8,128)}, u32[]{:S(2)}, u32[]{:S(2)}) async-start(f32[16,256,128]{2,1,0:T(8,128)} %get-tuple-element.57), calls=%async_computation.3 | async-start | bytes 4194304 | tf_op jit(solution)/shard_map/all_to_all | solution.py:354
  650.5 177.7 %all-gather.27.cloned.1.call-start = ((), (), s32[]{:S(2)}) async-start(), calls=%async_computation.14 | async-start | bytes 5242880 | tf_op jit(solution)/shard_map/all_gather | solution.py:374
  650.8 92.5 %collective-permute-start.24 = (f32[4096,128]{1,0:T(8,128)}, f32[4096,128]{1,0:T(8,128)S(1)}, u32[]{:S(2)}, u32[]{:S(2)}) collective-permute-start(f32[4096,128]{1,0:T(8,128)} %get-tuple-element.65.refs_0_), channel_id=1, source_target_pairs={{0,4},{1,5},{2,6},{3,7},{4,0},{5,1},{6,2},{7,3},{8,12},{9,13},{10,... | collective-permute-start | bytes 6291464 | tf_op jit(solution)/shard_map/ppermute | solution.py:369
  748.1 9.0 %collective-permute-start.25 = (f32[8,64,128]{2,1,0:T(8,128)}, f32[8,64,128]{2,1,0:T(8,128)S(1)}, u32[]{:S(2)}, u32[]{:S(2)}) collective-permute-start(f32[8,64,128]{2,1,0:T(8,128)} %get-tuple-element.96), channel_id=1, source_target_pairs={{0,1},{1,0},{2,3},{3,2},{4,5},{5,4},{6,7},{7,6},{8,9},{9,8},{10,11... | collective-permute-start | bytes 786440 | tf_op jit(solution)/shard_map/ppermute | solution.py:348
  749.8 8.6 %collective-permute-start.26 = (f32[8,64,128]{2,1,0:T(8,128)}, f32[8,64,128]{2,1,0:T(8,128)S(1)}, u32[]{:S(2)}, u32[]{:S(2)}) collective-permute-start(f32[8,64,128]{2,1,0:T(8,128)} %get-tuple-element.97), channel_id=1, source_target_pairs={{0,2},{1,3},{2,0},{3,1},{4,6},{5,7},{6,4},{7,5},{8,10},{9,11},{10,... | collective-permute-start | bytes 786440 | tf_op jit(solution)/shard_map/ppermute | solution.py:348
  749.8 11.5 %collective-permute-start.27 = (f32[8,64,128]{2,1,0:T(8,128)}, f32[8,64,128]{2,1,0:T(8,128)S(1)}, u32[]{:S(2)}, u32[]{:S(2)}) collective-permute-start(f32[8,64,128]{2,1,0:T(8,128)} %get-tuple-element.98), channel_id=1, source_target_pairs={{0,3},{1,2},{2,1},{3,0},{4,7},{5,6},{6,5},{7,4},{8,11},{9,10},{10,... | collective-permute-start | bytes 786440 | tf_op jit(solution)/shard_map/ppermute | solution.py:348
  763.4 82.1 %all-gather.25.cloned.1.call-start = ((), (), s32[]{:S(2)}) async-start(), calls=%async_computation.13 | async-start | bytes 2621440 | tf_op jit(solution)/shard_map/all_gather | solution.py:374
  763.4 45.0 %collective-permute-start = (f32[2048,128]{1,0:T(8,128)S(1)}, f32[2048,128]{1,0:T(8,128)S(1)}, u32[]{:S(2)}, u32[]{:S(2)}) collective-permute-start(f32[2048,128]{1,0:T(8,128)S(1)} %copy-done.6), channel_id=1, source_target_pairs={{0,4},{1,5},{2,6},{3,7},{4,0},{5,1},{6,2},{7,3},{8,12},{9,13},{10,... | collective-permute-start | bytes 3145736 | tf_op jit(solution)/shard_map/ppermute | solution.py:369
  812.1 5.7 collective-permute-start.21
  813.2 6.4 collective-permute-start.22
  813.3 8.4 collective-permute-start.23
  (11 other events, 52.4 us)
Sparse Core Ops, SparseCore 0:
  191.2 20.3 all-gather.14
  303.9 31.5 all-gather.18
  420.8 32.4 all-gather.16
  534.9 32.8 all-gather.22
  645.9 32.4 all-gather.20
  763.5 33.6 all-gather.26
  823.6 21.7 all-gather.24

commit v2 on v1

--- a/solution.py
+++ b/solution.py
@@ -47,7 +47,29 @@
     return jnp.where(lane < FRAMES, swapped, -swapped)
 
 
-def partial_kernel(cells_ref, *refs, senders, wide):
+def taken_kernel(*refs):
+    refs[-1][...] = refs[0][...]
+
+
+def taken(whole, start, size, after):
+    step = math.gcd(math.gcd(start, size), 8)
+    block = (step,) + whole.shape[1:]
+    return pl.pallas_call(
+        taken_kernel,
+        grid=(size // step,),
+        in_specs=[pl.BlockSpec(block, lambda i: (start // step + i, 0, 0))]
+        + [pl.BlockSpec(memory_space=pl.ANY)] * len(after),
+        out_specs=pl.BlockSpec(block, lambda i: (i, 0, 0)),
+        out_shape=jax.ShapeDtypeStruct((size,) + whole.shape[1:], whole.dtype),
+        compiler_params=pltpu.CompilerParams(vmem_limit_bytes=VMEM_LIMIT),
+        cost_estimate=pl.CostEstimate(
+            flops=0, bytes_accessed=2 * size * whole.size // whole.shape[0] * 4, transcendentals=0
+        ),
+        name="taken",
+    )(whole, *after)
+
+
+def partial_kernel(cells_ref, *refs, senders, start, wide):
     volts_ref, first_ref, second_ref = refs[:3]
     mine_ref, theirs_ref, grid_ref, rows_ref = refs[-4:]
     _, kc, feeds_each, _ = volts_ref.shape
@@ -70,8 +92,9 @@
         lax.fori_loop(0, feeds_each, place, 0, unroll=8)
 
     def one_channel(chan, _):
-        first = first_ref[chan]
-        second = second_ref[chan]
+        at_table = start + pl.program_id(0) * kc + chan
+        first = first_ref[at_table]
+        second = second_ref[at_table]
 
         def column_step(step, _):
             base = chan * cells + step * (wide * GRID)
@@ -112,14 +135,15 @@
     lax.fori_loop(0, kc, one_channel, 0)
 
 
-def partial_beams(cells, volts, first, second, kc, after, wide=4):
+def partial_beams(cells, volts, first, second, start, after, wide=4):
     senders, cc, feeds_each, _ = volts.shape
+    kc = cc if cc <= 8 else math.gcd(cc, 8)
     rows = SIDE // 2 * SIDE
     out = jax.ShapeDtypeStruct((cc * rows, LANES), jnp.float32)
-    table_spec = pl.BlockSpec((kc,) + first.shape[1:], lambda i, *_: (i, 0, 0))
+    table_spec = pl.BlockSpec(first.shape, lambda i, *_: (0, 0, 0))
     out_spec = pl.BlockSpec((kc * rows, LANES), lambda i, *_: (i, 0))
     return pl.pallas_call(
-        functools.partial(partial_kernel, senders=senders, wide=wide),
+        functools.partial(partial_kernel, senders=senders, start=start, wide=wide),
         grid_spec=pltpu.PrefetchScalarGridSpec(
             num_scalar_prefetch=1,
             grid=(cc // kc,),
@@ -137,9 +161,7 @@
         ),
         out_shape=[out, out],
         compiler_params=pltpu.CompilerParams(vmem_limit_bytes=VMEM_LIMIT),
-        cost_estimate=pl.CostEstimate(
-            flops=cc * 6 * 50_000_000, bytes_accessed=volts.size * 4 + 2 * cc * rows * LANES * 4, transcendentals=0
-        ),
+        cost_estimate=pl.CostEstimate(flops=int(cc * 3.9e9 * 10), bytes_accessed=0, transcendentals=0),
         name="partial_beams",
     )(cells, volts, first, second, *after)
 
@@ -204,14 +226,36 @@
         out_specs=[pl.BlockSpec((kc, each, LANES), lambda i: (i, 0, 0))] * owners,
         out_shape=[jax.ShapeDtypeStruct((cc, each, LANES), jnp.float32)] * owners,
         compiler_params=pltpu.CompilerParams(vmem_limit_bytes=VMEM_LIMIT),
-        cost_estimate=pl.CostEstimate(
-            flops=cc * rows * LANES * LANES * 3, bytes_accessed=mine.size * 12, transcendentals=0
-        ),
+        cost_estimate=pl.CostEstimate(flops=int(cc * 5e8 * 10), bytes_accessed=0, transcendentals=0),
         name="beam_spectra",
     )(mine, came, table, *after)
 
 
-def dedisperse_kernel(*refs, chans, each, trials, first, last):
+def joined_kernel(slots_ref, *refs, parts):
+    rows = refs[0].shape[0]
+    for j in range(parts):
+        refs[-1][pl.ds(slots_ref[j] * rows, rows)] = refs[j][...]
+
+
+def joined(slots, parts, after):
+    rows = parts[0].shape[0]
+    return pl.pallas_call(
+        functools.partial(joined_kernel, parts=len(parts)),
+        grid_spec=pltpu.PrefetchScalarGridSpec(
+            num_scalar_prefetch=1,
+            grid=(),
+            in_specs=[pl.BlockSpec(memory_space=pltpu.VMEM)] * len(parts)
+            + [pl.BlockSpec(memory_space=pl.ANY)] * len(after),
+            out_specs=pl.BlockSpec(memory_space=pltpu.VMEM),
+        ),
+        out_shape=jax.ShapeDtypeStruct((rows * len(parts),) + parts[0].shape[1:], jnp.float32),
+        compiler_params=pltpu.CompilerParams(vmem_limit_bytes=VMEM_LIMIT),
+        cost_estimate=pl.CostEstimate(flops=int(3e9 * 10), bytes_accessed=0, transcendentals=0),
+        name="joined",
+    )(slots, *parts, *after)
+
+
+def dedisperse_kernel(*refs, chans, each, trials, span, first, last):
     spectra_ref, cos_ref, sin_ref, inverse_ref = refs[:4]
     held_ref = None if first else refs[4]
     out_ref, bins_ref = refs[-3 if last else -2], refs[-1 if not last else -2]
@@ -231,7 +275,11 @@
 
     lax.fori_loop(0, chans // stack, turn_step, 0, unroll=4)
 
-    cos_one, sin_one = cos_ref[...], sin_ref[...]
+    turns = jnp.concatenate(
+        [ref[:, span, :].reshape(chans, trials) for ref in (cos_ref, sin_ref)], axis=1
+    )
+    turns = jnp.transpose(turns)
+    cos_one, sin_one = turns[:trials], turns[trials:]
 
     def bin_step(k, carry):
         cos_k, sin_k = carry
@@ -276,9 +324,9 @@
                 out_ref[pl.ds((step * wide + j) * FRAMES, FRAMES), :] = series[:, j * LANES : (j + 1) * LANES]
 
 
-def dedisperse(spectra, cos_one, sin_one, inverse, held, last):
-    each = spectra.shape[1]
-    trials, chans = cos_one.shape
+def dedisperse(spectra, cos_one, sin_one, span, inverse, held, last):
+    chans, each, _ = spectra.shape
+    trials = cos_one.shape[2]
     rows = trials * FRAMES
     args = [spectra.reshape(chans * each, LANES), cos_one, sin_one, inverse]
     if held is not None:
@@ -288,16 +336,14 @@
         scratch.append(pltpu.VMEM((rows, LANES), jnp.float32))
     return pl.pallas_call(
         functools.partial(
-            dedisperse_kernel, chans=chans, each=each, trials=trials, first=held is None, last=last
+            dedisperse_kernel, chans=chans, each=each, trials=trials, span=span, first=held is None, last=last
         ),
         in_specs=[pl.BlockSpec(memory_space=pltpu.VMEM)] * len(args),
         out_specs=pl.BlockSpec(memory_space=pltpu.VMEM),
         out_shape=jax.ShapeDtypeStruct((rows, LANES), jnp.float32),
         scratch_shapes=scratch,
         compiler_params=pltpu.CompilerParams(vmem_limit_bytes=VMEM_LIMIT),
-        cost_estimate=pl.CostEstimate(
-            flops=BINS * 2 * trials * chans * 2 * LANES * 6, bytes_accessed=spectra.size * 8, transcendentals=0
-        ),
+        cost_estimate=pl.CostEstimate(flops=int(1.3e10 * 10), bytes_accessed=0, transcendentals=0),
         name="dedisperse",
     )(*args)
 
@@ -334,8 +380,6 @@
 
     forward, inverse = forward_table(), inverse_table()
     trials = delays.shape[1] // bands
-    shifts = lax.all_to_all(delays, "band", split_axis=1, concat_axis=0, tiled=True)
-    shifts = shifts.reshape(bands, band_chans, trials)
 
     sizes = sizes_of(own_chans, CHUNK)
     starts = [sum(sizes[:i]) for i in range(len(sizes))]
@@ -347,37 +391,33 @@
     def swapped(part, step):
         return lax.ppermute(part, "feed", [(j, j ^ step) for j in range(devices)])
 
+    channels = jnp.concatenate(
+        [a * half + spot * cc + jnp.arange(cc, dtype=jnp.int32) for a, cc in zip(starts, sizes)]
+    ) + lax.axis_index("band") * band_chans
+    first = steering_tables(channels, natural)
+    second = steering_tables(channels, kept)
+
     def send_volts(i, *after):
-        piece = voltages[spans[i]]
-        if after:
-            piece = lax.optimization_barrier((piece,) + after)[0]
+        piece = taken(voltages, starts[i] * half, sizes[i] * half, after)
         volts[i] = lax.all_to_all(
             piece, "feed", split_axis=0, concat_axis=0, axis_index_groups=groups, tiled=True
         ).reshape(half, sizes[i], voltages.shape[1], LANES)
 
     def form_partial(i, *after):
-        cc = sizes[i]
-        channels = (
-            lax.axis_index("band") * band_chans
-            + starts[i] * half
-            + spot * cc
-            + jnp.arange(cc, dtype=jnp.int32)
-        )
-        first = steering_tables(channels, natural)
-        second = steering_tables(channels, kept)
-        mine[i], theirs[i] = partial_beams(cells, volts[i], first, second, math.gcd(cc, 8), after)
+        mine[i], theirs[i] = partial_beams(cells, volts[i], first, second, starts[i], after)
         came[i] = lax.ppermute(theirs[i], "feed", opposite)
 
     def form_spectra(i, *after):
         own = beam_spectra(mine[i], came[i], forward, half, split_rows, math.gcd(sizes[i], 4), after)
-        spectra[i] = jnp.concatenate([own[0]] + [swapped(own[step], step) for step in range(1, half)])
-        gathered[i] = lax.all_gather(spectra[i], "band")
+        spectra[i] = [own[0]] + [swapped(own[step], step) for step in range(1, half)]
+
+    def gather_spectra(i, *after):
+        gathered[i] = lax.all_gather(joined(partners, spectra[i], after), "band")
 
     def fold(i, held):
         each = gathered[i].shape[-2]
-        shift = shifts[:, spans[i]].reshape(bands, half, -1, trials)[:, partners].reshape(-1, trials).T.astype(jnp.float32) * (2.0 * math.pi / FRAMES)
         return dedisperse(
-            gathered[i].reshape(-1, each, LANES), jnp.cos(shift), jnp.sin(shift), inverse, held, i == count - 1
+            gathered[i].reshape(-1, each, LANES), shift_cos, shift_sin, spans[i], inverse, held, i == count - 1
         )
 
     for i in range(min(2, count)):
@@ -385,12 +425,19 @@
     for i in range(count + 3):
         if i < count:
             form_partial(i)
+        if i == 0:
+            shifts = lax.all_gather(delays, "band")
+            shifts = lax.dynamic_slice_in_dim(shifts, lax.axis_index("band") * trials, trials, 2)
+            shifts = shifts.astype(jnp.float32) * (2.0 * math.pi / FRAMES)
+            shift_cos, shift_sin = jnp.cos(shifts), jnp.sin(shifts)
         if i + 2 < count:
             send_volts(i + 2, theirs[i])
+        if 0 <= i - 2 < count:
+            gather_spectra(i - 2, *([theirs[i]] if i < count else []))
         if 0 <= i - 3 < count:
             held = fold(i - 3, held)
         if 0 <= i - 1 < count:
-            form_spectra(i - 1, *([theirs[i]] if i < count else []), *([held] if held is not None and i - 3 < count - 1 else []))
+            form_spectra(i - 1, *([theirs[i]] if i < count else []), *([held] if held is not None else []))
     each = gathered[0].shape[-2]
     return held.reshape(trials, FRAMES, LANES)[:, :, : 2 * each].swapaxes(1, 2)
 

time: 873 us -> 742 us (0.85)
  waiting for transfers between devices: 423 us -> 301 us
  Pallas kernels: 269 us -> 325 us
  local copies, waits for them, and re-layouts: 44.5 us -> 4.12 us
  other arithmetic: 41.6 us -> 15.9 us
    ppermute x7, waiting for transfers between devices: 264 us -> 32 us  [form_partial(): came[i] = lax.ppermute(theirs[i], 'feed', opposite)]
    all_to_all x7, waiting for transfers between devices: 78.7 us -> 218 us  [send_volts(): lax.all_to_all(piece, 'feed', split_axis=0, concat_axis=0, axis_index_gro...]
    pallas_call x7 -> x21, Pallas kernels: 159 us -> 214 us  [the longest x7 165 us: partial_beams(): pl.pallas_call(functools.partial(partial_kernel, senders=senders, start=s...]
    ppermute x21, waiting for transfers between devices: 74.9 us -> 43.3 us  [swapped(): return lax.ppermute(part, 'feed', [(j, j ^ step) for j in range(devices)])]
    slice x11 -> x0, local copies, waits for them, and re-layouts: 21 us -> none  [the longest x2 19.5 us: send_volts(): piece = voltages[spans[i]]]
    concatenate x7 -> x0, other arithmetic: 13.6 us -> none  [form_spectra(): jnp.concatenate([own[0]] + [swapped(own[step], step) for step in range(1,...]
  transfers between devices with their start and end apart: 43 -> 42, of which waited for: 32 -> 18; matrix products, arithmetic and copies ran while one was open for 9% -> 2% of each run, Pallas kernels for 30% -> 43%
where the time goes in v2:
time: 742 us; the launch traced here: 732 us
  Pallas kernels  325 us (44%)
  waiting for transfers between devices  301 us (41%)
  starting transfers between devices  63.2 us (9%)
  other arithmetic  15.9 us (2%)
  between operations  14.2 us (2%)
  blocking collectives  8.58 us (1%)
    all_to_all x7, waiting for transfers between devices, send_volts(): lax.all_to_all(piece, 'feed', split_axis=0, concat_axis=0, axis_index_gro...  218 us
    pallas_call x7, Pallas kernels, partial_beams(): pl.pallas_call(functools.partial(partial_kernel, senders=senders, start=s...  165 us
    pallas_call x7, Pallas kernels, dedisperse(): pl.pallas_call(functools.partial(dedisperse_kernel, chans=chans, each=eac...  88.2 us
    ppermute x21, waiting for transfers between devices, swapped(): return lax.ppermute(part, 'feed', [(j, j ^ step) for j in range(devices)])  43.3 us
    all_to_all x7, starting transfers between devices, send_volts(): lax.all_to_all(piece, 'feed', split_axis=0, concat_axis=0, axis_index_gro...  34.2 us
    ppermute x7, waiting for transfers between devices, form_partial(): came[i] = lax.ppermute(theirs[i], 'feed', opposite)  32 us
    pallas_call x7, Pallas kernels, taken(): pl.pallas_call(taken_kernel, grid=(size // step,), in_specs=[pl.BlockSpec...  29.2 us
    ppermute x21, starting transfers between devices, swapped(): return lax.ppermute(part, 'feed', [(j, j ^ step) for j in range(devices)])  25.2 us
  transfers between devices with their start and end apart: 42, of which 18 were waited for; matrix products, arithmetic and copies ran while one was open for 2% of the time, Pallas kernels for 43%

profile of v2, /device:TPU:0, one launch (start us, length us, event | category | flops | bytes accessed | tf_op | source)
XLA Modules:
  0.0 732.0 jit_solution(8120321661951042663)
XLA Ops:
  9.1 5.2 all-to-all-start
  15.1 4.8 taken.11
  23.2 8.6 %all-gather.1 = s32[768,256]{1,0:T(8,128)S(1)} all-gather(s32[192,256]{1,0:T(8,128)S(1)} %copy-done.1), channel_id=3, replica_groups=mesh['band'=4,'feed'=8] {'band'}, dimensions={0}, use_global_device_ids=true | all-gather | bytes 983040 | tf_op jit(solution)/shard_map/all_gather | solution.py:429
  34.1 6.4 fusion.9
  46.6 5.0 all-to-all-start.4
  51.6 15.3 %partial_beams.7 = (f32[2048,128]{1,0:T(8,128)}, f32[2048,128]{1,0:T(8,128)}) custom-call(s32[1024]{0:T(1024)} %dynamic_slice.6.cells_ref, f32[4,4,256,128]{3,2,1,0:T(8,128)} %bitcast.24, bf16[48,64,192]{2,1,0:T(8,128)(2,1)} %pad_maximum_fusion.1.refs_1_, bf16[48,64,192]{2,1,0:T(8,128)(2,1)} %pad_maximum_fusion.3.refs_2_), custom_call_target="tpu_custom_call" | custom-call | flops 155999993856 | tf_op jit(solution)/shard_map/partial_beams/pallas_call | solution.py:145
  66.9 4.8 taken.8
  74.3 48.3 %all-to-all-done.4 = f32[32,256,128]{2,1,0:T(8,128)} async-done(((f32[32,256,128]{2,1,0:T(8,128)}), f32[32,256,128]{2,1,0:T(8,128)}, u32[]{:S(2)}, u32[]{:S(2)}) %all-to-all-start.4) | async-done | bytes 4194336 | tf_op jit(solution)/shard_map/all_to_all | solution.py:402
  122.6 4.9 all-to-all-start.1
  127.4 26.8 %partial_beams.11 = (f32[4096,128]{1,0:T(8,128)}, f32[4096,128]{1,0:T(8,128)}) custom-call(s32[1024]{0:T(1024)} %dynamic_slice.6.cells_ref, f32[4,8,256,128]{3,2,1,0:T(8,128)} %bitcast.7.refs_0_, bf16[48,64,192]{2,1,0:T(8,128)(2,1)} %pad_maximum_fusion.1.refs_1_, bf16[48,64,192]{2,1,0:T(8,128)(2,1)} %pad_maximum_fusion.3.refs_2_), custom_call_target="tpu_custom_call" | custom-call | flops 311999987712 | tf_op jit(solution)/shard_map/partial_beams/pallas_call | solution.py:145
  154.7 4.8 taken.12
  166.4 27.2 %all-to-all-done.1 = f32[32,256,128]{2,1,0:T(8,128)} async-done(((f32[32,256,128]{2,1,0:T(8,128)}), f32[32,256,128]{2,1,0:T(8,128)}, u32[]{:S(2)}, u32[]{:S(2)}) %all-to-all-start.1) | async-done | bytes 4194336 | tf_op jit(solution)/shard_map/all_to_all | solution.py:402
  193.6 4.8 all-to-all-start.5
  198.5 26.8 %partial_beams.8 = (f32[4096,128]{1,0:T(8,128)}, f32[4096,128]{1,0:T(8,128)}) custom-call(s32[1024]{0:T(1024)} %dynamic_slice.6.cells_ref, f32[4,8,256,128]{3,2,1,0:T(8,128)} %bitcast.4.refs_0_, bf16[48,64,192]{2,1,0:T(8,128)(2,1)} %pad_maximum_fusion.1.refs_1_, bf16[48,64,192]{2,1,0:T(8,128)(2,1)} %pad_maximum_fusion.3.refs_2_), custom_call_target="tpu_custom_call" | custom-call | flops 311999987712 | tf_op jit(solution)/shard_map/partial_beams/pallas_call | solution.py:145
  225.3 4.8 taken.9
  230.1 18.9 %collective-permute-done.10.came_ref = f32[4096,128]{1,0:T(8,128)} collective-permute-done((f32[4096,128]{1,0:T(8,128)}, f32[4096,128]{1,0:T(8,128)}, u32[]{:S(2)}, u32[]{:S(2)}) %collective-permute-start.10) | collective-permute-done | bytes 2097184 | tf_op jit(solution)/shard_map/ppermute | solution.py:408
  249.0 3.4 beam_spectra.9
  258.6 39.2 %all-to-all-done.5 = f32[32,256,128]{2,1,0:T(8,128)} async-done(((f32[32,256,128]{2,1,0:T(8,128)}), f32[32,256,128]{2,1,0:T(8,128)}, u32[]{:S(2)}, u32[]{:S(2)}) %all-to-all-start.5) | async-done | bytes 4194336 | tf_op jit(solution)/shard_map/all_to_all | solution.py:402
  297.8 4.9 all-to-all-start.2
  302.9 26.9 %partial_beams.12 = (f32[4096,128]{1,0:T(8,128)}, f32[4096,128]{1,0:T(8,128)}) custom-call(s32[1024]{0:T(1024)} %dynamic_slice.6.cells_ref, f32[4,8,256,128]{3,2,1,0:T(8,128)} %bitcast.8.refs_0_, bf16[48,64,192]{2,1,0:T(8,128)(2,1)} %pad_maximum_fusion.1.refs_1_, bf16[48,64,192]{2,1,0:T(8,128)(2,1)} %pad_maximum_fusion.3.refs_2_), custom_call_target="tpu_custom_call" | custom-call | flops 311999987712 | tf_op jit(solution)/shard_map/partial_beams/pallas_call | solution.py:145
  329.8 4.8 taken.13
  337.6 9.2 %dedisperse.7.refs_1_.refs_4_ = f32[4096,128]{1,0:T(8,128)} custom-call(f32[4096,128]{1,0:T(8,128)} %bitcast.31, f32[4,192,64]{2,1,0:T(8,128)} %get-tuple-element.94.refs_1_, f32[4,192,64]{2,1,0:T(8,128)} %get-tuple-element.93.refs_2_, bf16[64,192]{1,0:T(8,128)(2,1)} %pad_maximum_fusion.6.refs_3_), custom_call_target="tpu_custom_call" | custom-call | flops 130000003072 | tf_op jit(solution)/shard_map/dedisperse/pallas_call | solution.py:337
  346.8 4.1 beam_spectra.8
  354.4 55.8 %all-to-all-done.2 = f32[32,256,128]{2,1,0:T(8,128)} async-done(((f32[32,256,128]{2,1,0:T(8,128)}), f32[32,256,128]{2,1,0:T(8,128)}, u32[]{:S(2)}, u32[]{:S(2)}) %all-to-all-start.2) | async-done | bytes 4194336 | tf_op jit(solution)/shard_map/all_to_all | solution.py:402
  410.2 4.9 all-to-all-start.6
  415.1 26.8 %partial_beams.9 = (f32[4096,128]{1,0:T(8,128)}, f32[4096,128]{1,0:T(8,128)}) custom-call(s32[1024]{0:T(1024)} %dynamic_slice.6.cells_ref, f32[4,8,256,128]{3,2,1,0:T(8,128)} %bitcast.5.refs_0_, bf16[48,64,192]{2,1,0:T(8,128)(2,1)} %pad_maximum_fusion.1.refs_1_, bf16[48,64,192]{2,1,0:T(8,128)(2,1)} %pad_maximum_fusion.3.refs_2_), custom_call_target="tpu_custom_call" | custom-call | flops 311999987712 | tf_op jit(solution)/shard_map/partial_beams/pallas_call | solution.py:145
  447.6 13.5 %dedisperse.8.refs_4_.refs_1_ = f32[4096,128]{1,0:T(8,128)} custom-call(f32[8192,128]{1,0:T(8,128)} %bitcast.27, f32[4,192,64]{2,1,0:T(8,128)} %get-tuple-element.94.refs_1_, f32[4,192,64]{2,1,0:T(8,128)} %get-tuple-element.93.refs_2_, bf16[64,192]{1,0:T(8,128)(2,1)} %pad_maximum_fusion.6.refs_3_, f32[4096,128]{1,0:T(8,128)} %dedisperse.7.refs_1_.refs_4_), custom_call_target="tpu_custom_call" | custom-call | flops 130000003072 | tf_op jit(solution)/shard_map/dedisperse/pallas_call | solution.py:337
  461.0 3.4 beam_spectra.11
  467.9 40.2 %all-to-all-done.6 = f32[32,256,128]{2,1,0:T(8,128)} async-done(((f32[32,256,128]{2,1,0:T(8,128)}), f32[32,256,128]{2,1,0:T(8,128)}, u32[]{:S(2)}, u32[]{:S(2)}) %all-to-all-start.6) | async-done | bytes 4194336 | tf_op jit(solution)/shard_map/all_to_all | solution.py:402
  508.2 4.5 all-to-all-start.3
  513.0 26.9 %partial_beams.13 = (f32[4096,128]{1,0:T(8,128)}, f32[4096,128]{1,0:T(8,128)}) custom-call(s32[1024]{0:T(1024)} %dynamic_slice.6.cells_ref, f32[4,8,256,128]{3,2,1,0:T(8,128)} %bitcast.9.refs_0_, bf16[48,64,192]{2,1,0:T(8,128)(2,1)} %pad_maximum_fusion.1.refs_1_, bf16[48,64,192]{2,1,0:T(8,128)(2,1)} %pad_maximum_fusion.3.refs_2_), custom_call_target="tpu_custom_call" | custom-call | flops 311999987712 | tf_op jit(solution)/shard_map/partial_beams/pallas_call | solution.py:145
  542.9 13.5 %dedisperse.9.refs_1_.refs_4_ = f32[4096,128]{1,0:T(8,128)} custom-call(f32[8192,128]{1,0:T(8,128)} %bitcast.26, f32[4,192,64]{2,1,0:T(8,128)} %get-tuple-element.94.refs_1_, f32[4,192,64]{2,1,0:T(8,128)} %get-tuple-element.93.refs_2_, bf16[64,192]{1,0:T(8,128)(2,1)} %pad_maximum_fusion.6.refs_3_, f32[4096,128]{1,0:T(8,128)} %dedisperse.8.refs_4_.refs_1_), custom_call_target="tpu_custom_call" | custom-call | flops 130000003072 | tf_op jit(solution)/shard_map/dedisperse/pallas_call | solution.py:337
  556.4 3.4 beam_spectra.10
  563.4 6.9 all-to-all-done.3
  570.3 15.4 %partial_beams.10 = (f32[2048,128]{1,0:T(8,128)}, f32[2048,128]{1,0:T(8,128)}) custom-call(s32[1024]{0:T(1024)} %dynamic_slice.6.cells_ref, f32[4,4,256,128]{3,2,1,0:T(8,128)} %bitcast.6.refs_0_, bf16[48,64,192]{2,1,0:T(8,128)(2,1)} %pad_maximum_fusion.1.refs_1_, bf16[48,64,192]{2,1,0:T(8,128)(2,1)} %pad_maximum_fusion.3.refs_2_), custom_call_target="tpu_custom_call" | custom-call | flops 155999993856 | tf_op jit(solution)/shard_map/partial_beams/pallas_call | solution.py:145
  585.7 15.4 %collective-permute-done.15.refs_2_ = f32[8,64,128]{2,1,0:T(8,128)} collective-permute-done((f32[8,64,128]{2,1,0:T(8,128)}, f32[8,64,128]{2,1,0:T(8,128)}, u32[]{:S(2)}, u32[]{:S(2)}) %collective-permute-start.15) | collective-permute-done | bytes 262176 | tf_op jit(solution)/shard_map/ppermute | solution.py:392
  601.0 4.7 collective-permute-done.16.refs_3_
  608.8 13.5 %dedisperse.10.refs_4_.refs_1_ = f32[4096,128]{1,0:T(8,128)} custom-call(f32[8192,128]{1,0:T(8,128)} %bitcast.28, f32[4,192,64]{2,1,0:T(8,128)} %get-tuple-element.94.refs_1_, f32[4,192,64]{2,1,0:T(8,128)} %get-tuple-element.93.refs_2_, bf16[64,192]{1,0:T(8,128)(2,1)} %pad_maximum_fusion.6.refs_3_, f32[4096,128]{1,0:T(8,128)} %dedisperse.9.refs_1_.refs_4_), custom_call_target="tpu_custom_call" | custom-call | flops 130000003072 | tf_op jit(solution)/shard_map/dedisperse/pallas_call | solution.py:337
  622.3 5.0 collective-permute-done.24.came_ref
  627.2 3.4 beam_spectra.13
  634.2 3.1 collective-permute-done.25.refs_1_
  637.2 10.7 %collective-permute-done.26.refs_2_ = f32[8,64,128]{2,1,0:T(8,128)S(1)} collective-permute-done((f32[8,64,128]{2,1,0:T(8,128)}, f32[8,64,128]{2,1,0:T(8,128)S(1)}, u32[]{:S(2)}, u32[]{:S(2)}) %collective-permute-start.26) | collective-permute-done | bytes 262176 | tf_op jit(solution)/shard_map/ppermute | solution.py:392
  648.0 4.9 collective-permute-done.27.refs_3_
  656.5 13.5 %dedisperse.11.refs_0_.refs_4_ = f32[4096,128]{1,0:T(8,128)} custom-call(f32[8192,128]{1,0:T(8,128)} %bitcast.29, f32[4,192,64]{2,1,0:T(8,128)} %get-tuple-element.94.refs_1_, f32[4,192,64]{2,1,0:T(8,128)} %get-tuple-element.93.refs_2_, bf16[64,192]{1,0:T(8,128)(2,1)} %pad_maximum_fusion.6.refs_3_, f32[4096,128]{1,0:T(8,128)} %dedisperse.10.refs_4_.refs_1_), custom_call_target="tpu_custom_call" | custom-call | flops 130000003072 | tf_op jit(solution)/shard_map/dedisperse/pallas_call | solution.py:337
  670.0 8.1 %collective-permute-done.came_ref = f32[2048,128]{1,0:T(8,128)} collective-permute-done((f32[2048,128]{1,0:T(8,128)}, f32[2048,128]{1,0:T(8,128)}, u32[]{:S(2)}, u32[]{:S(2)}) %collective-permute-start) | collective-permute-done | bytes 1048608 | tf_op jit(solution)/shard_map/ppermute | solution.py:408
  692.3 13.6 %dedisperse.12.refs_4_ = f32[4096,128]{1,0:T(8,128)} custom-call(f32[8192,128]{1,0:T(8,128)} %bitcast.30, f32[4,192,64]{2,1,0:T(8,128)} %get-tuple-element.94.refs_1_, f32[4,192,64]{2,1,0:T(8,128)} %get-tuple-element.93.refs_2_, bf16[64,192]{1,0:T(8,128)(2,1)} %pad_maximum_fusion.6.refs_3_, f32[4096,128]{1,0:T(8,128)} %dedisperse.11.refs_0_.refs_4_), custom_call_target="tpu_custom_call" | custom-call | flops 130000003072 | tf_op jit(solution)/shard_map/dedisperse/pallas_call | solution.py:337
  705.8 7.4 %all-gather.26.cloned.1.call-done = f32[64,64,128]{2,1,0:T(8,128)} async-done(((f32[16,64,128]{2,1,0:T(8,128)}), f32[64,64,128]{2,1,0:T(8,128)}) %all-gather.26.cloned.1.call-update) | async-done | bytes 2097168 | tf_op jit(solution)/shard_map/all_gather | solution.py:415
  713.2 11.5 %dedisperse.13 = f32[4096,128]{1,0:T(8,128)} custom-call(f32[4096,128]{1,0:T(8,128)} %bitcast.32, f32[4,192,64]{2,1,0:T(8,128)} %get-tuple-element.94.refs_1_, f32[4,192,64]{2,1,0:T(8,128)} %get-tuple-element.93.refs_2_, bf16[64,192]{1,0:T(8,128)(2,1)} %pad_maximum_fusion.6.refs_3_, f32[4096,128]{1,0:T(8,128)} %dedisperse.12.refs_4_), custom_call_target="tpu_custom_call" | custom-call | flops 130000003072 | tf_op jit(solution)/shard_map/dedisperse/pallas_call | solution.py:337
  (131 shorter events, 78.0 us)
Async XLA Ops:
  9.1 36.1 %all-to-all-start = ((f32[16,256,128]{2,1,0:T(8,128)}), f32[16,256,128]{2,1,0:T(8,128)S(1)}, u32[]{:S(2)}, u32[]{:S(2)}) async-start(f32[16,256,128]{2,1,0:T(8,128)} %taken.7), calls=%async_computation | async-start | bytes 4194304 | tf_op jit(solution)/shard_map/all_to_all | solution.py:402
  15.1 5.0 slice-start
  15.1 8.1 %copy-start.1 = (s32[192,256]{1,0:T(8,128)S(1)}, s32[192,256]{1,0:T(8,128)}, u32[]{:S(2)}) copy-start(s32[192,256]{1,0:T(8,128)} %param.5) | copy-start | bytes 589828
  46.6 76.0 %all-to-all-start.4 = ((f32[32,256,128]{2,1,0:T(8,128)}), f32[32,256,128]{2,1,0:T(8,128)}, u32[]{:S(2)}, u32[]{:S(2)}) async-start(f32[32,256,128]{2,1,0:T(8,128)} %taken.11), calls=%async_computation.4 | async-start | bytes 8388608 | tf_op jit(solution)/shard_map/all_to_all | solution.py:402
  71.7 87.7 %collective-permute-start.3 = (f32[2048,128]{1,0:T(8,128)}, f32[2048,128]{1,0:T(8,128)}, u32[]{:S(2)}, u32[]{:S(2)}) collective-permute-start(f32[2048,128]{1,0:T(8,128)} %get-tuple-element.47.refs_1_), channel_id=1, source_target_pairs={{0,4},{1,5},{2,6},{3,7},{4,0},{5,1},{6,2},{7,3},{8,12},{9,13},{10,... | collective-permute-start | bytes 3145736 | tf_op jit(solution)/shard_map/ppermute | solution.py:408
  122.6 71.0 %all-to-all-start.1 = ((f32[32,256,128]{2,1,0:T(8,128)}), f32[32,256,128]{2,1,0:T(8,128)}, u32[]{:S(2)}, u32[]{:S(2)}) async-start(f32[32,256,128]{2,1,0:T(8,128)} %taken.8), calls=%async_computation.1 | async-start | bytes 8388608 | tf_op jit(solution)/shard_map/all_to_all | solution.py:402
  154.2 94.8 %collective-permute-start.10 = (f32[4096,128]{1,0:T(8,128)}, f32[4096,128]{1,0:T(8,128)}, u32[]{:S(2)}, u32[]{:S(2)}) collective-permute-start(f32[4096,128]{1,0:T(8,128)} %get-tuple-element.53.refs_1_.refs_0_), channel_id=1, source_target_pairs={{0,4},{1,5},{2,6},{3,7},{4,0},{5,1},{6,2},{7,3},{8,12},{9,13},{10,... | collective-permute-start | bytes 6291464 | tf_op jit(solution)/shard_map/ppermute | solution.py:408
  162.2 92.2 %collective-permute-start.4 = (f32[4,64,128]{2,1,0:T(8,128)}, f32[4,64,128]{2,1,0:T(8,128)}, u32[]{:S(2)}, u32[]{:S(2)}) collective-permute-start(f32[4,64,128]{2,1,0:T(8,128)} %get-tuple-element.59), channel_id=1, source_target_pairs={{0,1},{1,0},{2,3},{3,2},{4,5},{5,4},{6,7},{7,6},{8,9},{9,8},{10,11... | collective-permute-start | bytes 393224 | tf_op jit(solution)/shard_map/ppermute | solution.py:392
  164.2 90.2 %collective-permute-start.5 = (f32[4,64,128]{2,1,0:T(8,128)}, f32[4,64,128]{2,1,0:T(8,128)}, u32[]{:S(2)}, u32[]{:S(2)}) collective-permute-start(f32[4,64,128]{2,1,0:T(8,128)} %get-tuple-element.60), channel_id=1, source_target_pairs={{0,2},{1,3},{2,0},{3,1},{4,6},{5,7},{6,4},{7,5},{8,10},{9,11},{10,... | collective-permute-start | bytes 393224 | tf_op jit(solution)/shard_map/ppermute | solution.py:392
  166.4 89.6 %collective-permute-start.6 = (f32[4,64,128]{2,1,0:T(8,128)}, f32[4,64,128]{2,1,0:T(8,128)}, u32[]{:S(2)}, u32[]{:S(2)}) collective-permute-start(f32[4,64,128]{2,1,0:T(8,128)} %get-tuple-element.61), channel_id=1, source_target_pairs={{0,3},{1,2},{2,1},{3,0},{4,7},{5,6},{6,5},{7,4},{8,11},{9,10},{10,... | collective-permute-start | bytes 393224 | tf_op jit(solution)/shard_map/ppermute | solution.py:392
  193.6 104.2 %all-to-all-start.5 = ((f32[32,256,128]{2,1,0:T(8,128)}), f32[32,256,128]{2,1,0:T(8,128)}, u32[]{:S(2)}, u32[]{:S(2)}) async-start(f32[32,256,128]{2,1,0:T(8,128)} %taken.12), calls=%async_computation.5 | async-start | bytes 8388608 | tf_op jit(solution)/shard_map/all_to_all | solution.py:402
  198.4 139.2 %all-gather.16.cloned.1.call-start = ((), (), s32[]{:S(2)}) async-start(), calls=%async_computation.7 | async-start | bytes 2621440 | tf_op jit(solution)/shard_map/all_gather | solution.py:415
  230.1 116.6 %collective-permute-start.2 = (f32[4096,128]{1,0:T(8,128)}, f32[4096,128]{1,0:T(8,128)}, u32[]{:S(2)}, u32[]{:S(2)}) collective-permute-start(f32[4096,128]{1,0:T(8,128)} %get-tuple-element.48.refs_1_.refs_4_.refs_0_), channel_id=1, source_target_pairs={{0,4},{1,5},{2,6},{3,7},{4,0},{5,1},{6,2},{7,3},{8,12},{9,13},{10,... | collective-permute-start | bytes 6291464 | tf_op jit(solution)/shard_map/ppermute | solution.py:408
  252.4 82.2 %collective-permute-start.11 = (f32[8,64,128]{2,1,0:T(8,128)}, f32[8,64,128]{2,1,0:T(8,128)}, u32[]{:S(2)}, u32[]{:S(2)}) collective-permute-start(f32[8,64,128]{2,1,0:T(8,128)} %get-tuple-element.68), channel_id=1, source_target_pairs={{0,1},{1,0},{2,3},{3,2},{4,5},{5,4},{6,7},{7,6},{8,9},{9,8},{10,11... | collective-permute-start | bytes 786440 | tf_op jit(solution)/shard_map/ppermute | solution.py:392
  254.4 80.2 %collective-permute-start.12 = (f32[8,64,128]{2,1,0:T(8,128)}, f32[8,64,128]{2,1,0:T(8,128)}, u32[]{:S(2)}, u32[]{:S(2)}) collective-permute-start(f32[8,64,128]{2,1,0:T(8,128)} %get-tuple-element.69), channel_id=1, source_target_pairs={{0,2},{1,3},{2,0},{3,1},{4,6},{5,7},{6,4},{7,5},{8,10},{9,11},{10,... | collective-permute-start | bytes 786440 | tf_op jit(solution)/shard_map/ppermute | solution.py:392
  254.5 80.2 %collective-permute-start.13 = (f32[8,64,128]{2,1,0:T(8,128)}, f32[8,64,128]{2,1,0:T(8,128)}, u32[]{:S(2)}, u32[]{:S(2)}) collective-permute-start(f32[8,64,128]{2,1,0:T(8,128)} %get-tuple-element.70), channel_id=1, source_target_pairs={{0,3},{1,2},{2,1},{3,0},{4,7},{5,6},{6,5},{7,4},{8,11},{9,10},{10,... | collective-permute-start | bytes 786440 | tf_op jit(solution)/shard_map/ppermute | solution.py:392
  297.8 112.4 %all-to-all-start.2 = ((f32[32,256,128]{2,1,0:T(8,128)}), f32[32,256,128]{2,1,0:T(8,128)}, u32[]{:S(2)}, u32[]{:S(2)}) async-start(f32[32,256,128]{2,1,0:T(8,128)} %taken.9), calls=%async_computation.2 | async-start | bytes 8388608 | tf_op jit(solution)/shard_map/all_to_all | solution.py:402
  302.7 144.9 %all-gather.20.cloned.1.call-start = ((), (), s32[]{:S(2)}) async-start(), calls=%async_computation.9 | async-start | bytes 5242880 | tf_op jit(solution)/shard_map/all_gather | solution.py:415
  329.8 131.2 %collective-permute-start.17 = (f32[4096,128]{1,0:T(8,128)}, f32[4096,128]{1,0:T(8,128)}, u32[]{:S(2)}, u32[]{:S(2)}) collective-permute-start(f32[4096,128]{1,0:T(8,128)} %get-tuple-element.54.refs_1_.refs_0_.refs_4_), channel_id=1, source_target_pairs={{0,4},{1,5},{2,6},{3,7},{4,0},{5,1},{6,2},{7,3},{8,12},{9,13},{10,... | collective-permute-start | bytes 6291464 | tf_op jit(solution)/shard_map/ppermute | solution.py:408
  350.9 93.7 %collective-permute-start.7 = (f32[8,64,128]{2,1,0:T(8,128)}, f32[8,64,128]{2,1,0:T(8,128)}, u32[]{:S(2)}, u32[]{:S(2)}) collective-permute-start(f32[8,64,128]{2,1,0:T(8,128)} %get-tuple-element.63), channel_id=1, source_target_pairs={{0,1},{1,0},{2,3},{3,2},{4,5},{5,4},{6,7},{7,6},{8,9},{9,8},{10,11... | collective-permute-start | bytes 786440 | tf_op jit(solution)/shard_map/ppermute | solution.py:392
  352.8 91.8 %collective-permute-start.8 = (f32[8,64,128]{2,1,0:T(8,128)}, f32[8,64,128]{2,1,0:T(8,128)}, u32[]{:S(2)}, u32[]{:S(2)}) collective-permute-start(f32[8,64,128]{2,1,0:T(8,128)} %get-tuple-element.64), channel_id=1, source_target_pairs={{0,2},{1,3},{2,0},{3,1},{4,6},{5,7},{6,4},{7,5},{8,10},{9,11},{10,... | collective-permute-start | bytes 786440 | tf_op jit(solution)/shard_map/ppermute | solution.py:392
  354.3 90.3 %collective-permute-start.9 = (f32[8,64,128]{2,1,0:T(8,128)}, f32[8,64,128]{2,1,0:T(8,128)}, u32[]{:S(2)}, u32[]{:S(2)}) collective-permute-start(f32[8,64,128]{2,1,0:T(8,128)} %get-tuple-element.65), channel_id=1, source_target_pairs={{0,3},{1,2},{2,1},{3,0},{4,7},{5,6},{6,5},{7,4},{8,11},{9,10},{10,... | collective-permute-start | bytes 786440 | tf_op jit(solution)/shard_map/ppermute | solution.py:392
  410.2 98.0 %all-to-all-start.6 = ((f32[32,256,128]{2,1,0:T(8,128)}), f32[32,256,128]{2,1,0:T(8,128)}, u32[]{:S(2)}, u32[]{:S(2)}) async-start(f32[32,256,128]{2,1,0:T(8,128)} %taken.13), calls=%async_computation.6 | async-start | bytes 8388608 | tf_op jit(solution)/shard_map/all_to_all | solution.py:402
  415.1 127.8 %all-gather.18.cloned.1.call-start = ((), (), s32[]{:S(2)}) async-start(), calls=%async_computation.8 | async-start | bytes 5242880 | tf_op jit(solution)/shard_map/all_gather | solution.py:415
  444.6 111.9 %collective-permute-start.1 = (f32[4096,128]{1,0:T(8,128)}, f32[4096,128]{1,0:T(8,128)}, u32[]{:S(2)}, u32[]{:S(2)}) collective-permute-start(f32[4096,128]{1,0:T(8,128)} %get-tuple-element.49.refs_1_.refs_4_.refs_0_), channel_id=1, source_target_pairs={{0,4},{1,5},{2,6},{3,7},{4,0},{5,1},{6,2},{7,3},{8,12},{9,13},{10,... | collective-permute-start | bytes 6291464 | tf_op jit(solution)/shard_map/ppermute | solution.py:408
  464.5 75.4 %collective-permute-start.18 = (f32[8,64,128]{2,1,0:T(8,128)}, f32[8,64,128]{2,1,0:T(8,128)}, u32[]{:S(2)}, u32[]{:S(2)}) collective-permute-start(f32[8,64,128]{2,1,0:T(8,128)} %get-tuple-element.77), channel_id=1, source_target_pairs={{0,1},{1,0},{2,3},{3,2},{4,5},{5,4},{6,7},{7,6},{8,9},{9,8},{10,11... | collective-permute-start | bytes 786440 | tf_op jit(solution)/shard_map/ppermute | solution.py:392
  466.4 73.5 %collective-permute-start.19 = (f32[8,64,128]{2,1,0:T(8,128)}, f32[8,64,128]{2,1,0:T(8,128)}, u32[]{:S(2)}, u32[]{:S(2)}) collective-permute-start(f32[8,64,128]{2,1,0:T(8,128)} %get-tuple-element.78), channel_id=1, source_target_pairs={{0,2},{1,3},{2,0},{3,1},{4,6},{5,7},{6,4},{7,5},{8,10},{9,11},{10,... | collective-permute-start | bytes 786440 | tf_op jit(solution)/shard_map/ppermute | solution.py:392
  467.9 72.0 %collective-permute-start.20 = (f32[8,64,128]{2,1,0:T(8,128)}, f32[8,64,128]{2,1,0:T(8,128)}, u32[]{:S(2)}, u32[]{:S(2)}) collective-permute-start(f32[8,64,128]{2,1,0:T(8,128)} %get-tuple-element.79), channel_id=1, source_target_pairs={{0,3},{1,2},{2,1},{3,0},{4,7},{5,6},{6,5},{7,4},{8,11},{9,10},{10,... | collective-permute-start | bytes 786440 | tf_op jit(solution)/shard_map/ppermute | solution.py:392
  508.2 62.1 %all-to-all-start.3 = ((f32[16,256,128]{2,1,0:T(8,128)}), f32[16,256,128]{2,1,0:T(8,128)}, u32[]{:S(2)}, u32[]{:S(2)}) async-start(f32[16,256,128]{2,1,0:T(8,128)} %taken.10), calls=%async_computation.3 | async-start | bytes 4194304 | tf_op jit(solution)/shard_map/all_to_all | solution.py:402
  512.7 96.1 %all-gather.24.cloned.1.call-start = ((), (), s32[]{:S(2)}) async-start(), calls=%async_computation.11 | async-start | bytes 5242880 | tf_op jit(solution)/shard_map/all_gather | solution.py:415
  539.9 87.4 %collective-permute-start.24 = (f32[4096,128]{1,0:T(8,128)}, f32[4096,128]{1,0:T(8,128)}, u32[]{:S(2)}, u32[]{:S(2)}) collective-permute-start(f32[4096,128]{1,0:T(8,128)} %get-tuple-element.55.refs_0_.refs_4_), channel_id=1, source_target_pairs={{0,4},{1,5},{2,6},{3,7},{4,0},{5,1},{6,2},{7,3},{8,12},{9,13},{10,... | collective-permute-start | bytes 6291464 | tf_op jit(solution)/shard_map/ppermute | solution.py:408
  542.8 113.7 %all-gather.22.cloned.1.call-start = ((), (), s32[]{:S(2)}) async-start(), calls=%async_computation.10 | async-start | bytes 5242880 | tf_op jit(solution)/shard_map/all_gather | solution.py:415
  559.9 25.8 %collective-permute-start.14 = (f32[8,64,128]{2,1,0:T(8,128)}, f32[8,64,128]{2,1,0:T(8,128)}, u32[]{:S(2)}, u32[]{:S(2)}) collective-permute-start(f32[8,64,128]{2,1,0:T(8,128)} %get-tuple-element.72), channel_id=1, source_target_pairs={{0,1},{1,0},{2,3},{3,2},{4,5},{5,4},{6,7},{7,6},{8,9},{9,8},{10,11... | collective-permute-start | bytes 786440 | tf_op jit(solution)/shard_map/ppermute | solution.py:392
  561.8 39.2 %collective-permute-start.15 = (f32[8,64,128]{2,1,0:T(8,128)}, f32[8,64,128]{2,1,0:T(8,128)}, u32[]{:S(2)}, u32[]{:S(2)}) collective-permute-start(f32[8,64,128]{2,1,0:T(8,128)} %get-tuple-element.73), channel_id=1, source_target_pairs={{0,2},{1,3},{2,0},{3,1},{4,6},{5,7},{6,4},{7,5},{8,10},{9,11},{10,... | collective-permute-start | bytes 786440 | tf_op jit(solution)/shard_map/ppermute | solution.py:392
  563.3 42.5 %collective-permute-start.16 = (f32[8,64,128]{2,1,0:T(8,128)}, f32[8,64,128]{2,1,0:T(8,128)}, u32[]{:S(2)}, u32[]{:S(2)}) collective-permute-start(f32[8,64,128]{2,1,0:T(8,128)} %get-tuple-element.74), channel_id=1, source_target_pairs={{0,3},{1,2},{2,1},{3,0},{4,7},{5,6},{6,5},{7,4},{8,11},{9,10},{10,... | collective-permute-start | bytes 786440 | tf_op jit(solution)/shard_map/ppermute | solution.py:392
  608.7 83.5 %all-gather.28.cloned.1.call-start = ((), (), s32[]{:S(2)}) async-start(), calls=%async_computation.13 | async-start | bytes 5242880 | tf_op jit(solution)/shard_map/all_gather | solution.py:415
  630.7 6.6 collective-permute-start.25
  632.4 15.6 %collective-permute-start.26 = (f32[8,64,128]{2,1,0:T(8,128)}, f32[8,64,128]{2,1,0:T(8,128)S(1)}, u32[]{:S(2)}, u32[]{:S(2)}) collective-permute-start(f32[8,64,128]{2,1,0:T(8,128)} %get-tuple-element.87), channel_id=1, source_target_pairs={{0,2},{1,3},{2,0},{3,1},{4,6},{5,7},{6,4},{7,5},{8,10},{9,11},{10,... | collective-permute-start | bytes 786440 | tf_op jit(solution)/shard_map/ppermute | solution.py:392
  632.4 20.5 %collective-permute-start.27 = (f32[8,64,128]{2,1,0:T(8,128)}, f32[8,64,128]{2,1,0:T(8,128)S(1)}, u32[]{:S(2)}, u32[]{:S(2)}) collective-permute-start(f32[8,64,128]{2,1,0:T(8,128)} %get-tuple-element.88), channel_id=1, source_target_pairs={{0,3},{1,2},{2,1},{3,0},{4,7},{5,6},{6,5},{7,4},{8,11},{9,10},{10,... | collective-permute-start | bytes 786440 | tf_op jit(solution)/shard_map/ppermute | solution.py:392
  634.2 44.0 %collective-permute-start = (f32[2048,128]{1,0:T(8,128)}, f32[2048,128]{1,0:T(8,128)}, u32[]{:S(2)}, u32[]{:S(2)}) collective-permute-start(f32[2048,128]{1,0:T(8,128)} %get-tuple-element.51.refs_4_.refs_0_), channel_id=1, source_target_pairs={{0,4},{1,5},{2,6},{3,7},{4,0},{5,1},{6,2},{7,3},{8,12},{9,13},{10,... | collective-permute-start | bytes 3145736 | tf_op jit(solution)/shard_map/ppermute | solution.py:408
  637.2 15.6 %copy-start.2 = (f32[8,64,128]{2,1,0:T(8,128)}, f32[8,64,128]{2,1,0:T(8,128)S(1)}, u32[]{:S(2)}) copy-start(f32[8,64,128]{2,1,0:T(8,128)S(1)} %collective-permute-done.25.refs_1_) | copy-start | bytes 786436
  648.0 4.9 copy-start.3
  656.5 56.7 %all-gather.26.cloned.1.call-start = ((), (), s32[]{:S(2)}) async-start(), calls=%async_computation.12 | async-start | bytes 2621440 | tf_op jit(solution)/shard_map/all_gather | solution.py:415
  680.9 5.2 collective-permute-start.21
  681.3 5.2 collective-permute-start.22
  681.3 7.6 %collective-permute-start.23 = (f32[4,64,128]{2,1,0:T(8,128)}, f32[4,64,128]{2,1,0:T(8,128)S(1)}, u32[]{:S(2)}, u32[]{:S(2)}) collective-permute-start(f32[4,64,128]{2,1,0:T(8,128)} %get-tuple-element.83), channel_id=1, source_target_pairs={{0,3},{1,2},{2,1},{3,0},{4,7},{5,6},{6,5},{7,4},{8,11},{9,10},{10,... | collective-permute-start | bytes 393224 | tf_op jit(solution)/shard_map/ppermute | solution.py:392
  686.1 2.9 copy-start.5
  686.5 2.5 copy-start.6
  (3 other events, 2.7 us)
Sparse Core Ops, SparseCore 0:
  258.8 21.8 all-gather.15
  337.7 36.3 all-gather.19
  447.7 36.3 all-gather.17
  542.9 36.3 all-gather.23
  608.8 34.7 all-gather.21
  656.6 31.5 all-gather.27
  692.4 20.7 all-gather.25

commit v3 on v2

--- a/solution.py
+++ b/solution.py
@@ -16,7 +16,6 @@
 GRID = 64
 BINS = FRAMES // 2
 LANES = 2 * FRAMES
-CHUNK = 8
 VMEM_LIMIT = 56 * 1024 * 1024
 
 
@@ -161,7 +160,7 @@
         ),
         out_shape=[out, out],
         compiler_params=pltpu.CompilerParams(vmem_limit_bytes=VMEM_LIMIT),
-        cost_estimate=pl.CostEstimate(flops=int(cc * 3.9e9 * 10), bytes_accessed=0, transcendentals=0),
+        cost_estimate=pl.CostEstimate(flops=int(cc * 3.9e10), bytes_accessed=0, transcendentals=0),
         name="partial_beams",
     )(cells, volts, first, second, *after)
 
@@ -226,7 +225,7 @@
         out_specs=[pl.BlockSpec((kc, each, LANES), lambda i: (i, 0, 0))] * owners,
         out_shape=[jax.ShapeDtypeStruct((cc, each, LANES), jnp.float32)] * owners,
         compiler_params=pltpu.CompilerParams(vmem_limit_bytes=VMEM_LIMIT),
-        cost_estimate=pl.CostEstimate(flops=int(cc * 5e8 * 10), bytes_accessed=0, transcendentals=0),
+        cost_estimate=pl.CostEstimate(flops=int(cc * 5e9), bytes_accessed=0, transcendentals=0),
         name="beam_spectra",
     )(mine, came, table, *after)
 
@@ -250,7 +249,7 @@
         ),
         out_shape=jax.ShapeDtypeStruct((rows * len(parts),) + parts[0].shape[1:], jnp.float32),
         compiler_params=pltpu.CompilerParams(vmem_limit_bytes=VMEM_LIMIT),
-        cost_estimate=pl.CostEstimate(flops=int(3e9 * 10), bytes_accessed=0, transcendentals=0),
+        cost_estimate=pl.CostEstimate(flops=int(3e10), bytes_accessed=0, transcendentals=0),
         name="joined",
     )(slots, *parts, *after)
 
@@ -273,7 +272,7 @@
             bins_ref[pl.ds(step * stack + e, FRAMES, stride=chans), :] = jnp.where(lane < each, left, right)
         return 0
 
-    lax.fori_loop(0, chans // stack, turn_step, 0, unroll=4)
+    lax.fori_loop(0, chans // stack, turn_step, 0, unroll=min(16, chans // stack) if last else 4)
 
     turns = jnp.concatenate(
         [ref[:, span, :].reshape(chans, trials) for ref in (cos_ref, sin_ref)], axis=1
@@ -308,7 +307,7 @@
         total_ref[at_imag, :] = imag
         return cos_k * cos_one - sin_k * sin_one, sin_k * cos_one + cos_k * sin_one
 
-    lax.fori_loop(0, BINS, bin_step, (cos_one, sin_one), unroll=4)
+    lax.fori_loop(0, BINS, bin_step, (cos_one, sin_one), unroll=True if last else 4)
 
     if last:
         wide = 4
@@ -343,16 +342,18 @@
         out_shape=jax.ShapeDtypeStruct((rows, LANES), jnp.float32),
         scratch_shapes=scratch,
         compiler_params=pltpu.CompilerParams(vmem_limit_bytes=VMEM_LIMIT),
-        cost_estimate=pl.CostEstimate(flops=int(1.3e10 * 10), bytes_accessed=0, transcendentals=0),
+        cost_estimate=pl.CostEstimate(flops=int(1.3e11), bytes_accessed=0, transcendentals=0),
         name="dedisperse",
     )(*args)
 
 
-def sizes_of(total, step):
-    if total < 2 * step or total % step or step % 2:
-        step = math.gcd(total, max(step // 2, 1))
-        return [step] * (total // step)
-    return [step // 2] + [step] * (total // step - 1) + [step // 2]
+def sizes_of(total, half):
+    shares = (2, 4, 4, 4, 4, 3, 2, 1)
+    unit, rest = divmod(total, sum(shares))
+    if unit and not rest and unit * half % 8 == 0:
+        return [unit * share for share in shares]
+    step = math.gcd(total, 4)
+    return [step] * (total // step)
 
 
 def body(voltages, feed_cells, delays):
@@ -381,7 +382,7 @@
     forward, inverse = forward_table(), inverse_table()
     trials = delays.shape[1] // bands
 
-    sizes = sizes_of(own_chans, CHUNK)
+    sizes = sizes_of(own_chans, half)
     starts = [sum(sizes[:i]) for i in range(len(sizes))]
     spans = [slice(a * half, (a + cc) * half) for a, cc in zip(starts, sizes)]
     count = len(sizes)

time: 742 us -> 739 us (level)
  waiting for transfers between devices: 301 us -> 275 us
  Pallas kernels: 325 us -> 340 us
  starting transfers between devices: 63.2 us -> 71.1 us
    ppermute x21 -> x24, waiting for transfers between devices: 43.3 us -> 17.1 us  [swapped(): return lax.ppermute(part, 'feed', [(j, j ^ step) for j in range(devices)])]
    ppermute x7 -> x8, waiting for transfers between devices: 32 us -> 50.4 us  [form_partial(): came[i] = lax.ppermute(theirs[i], 'feed', opposite)]
    all_to_all x7 -> x8, waiting for transfers between devices: 218 us -> 201 us  [send_volts(): lax.all_to_all(piece, 'feed', split_axis=0, concat_axis=0, axis_index_gro...]
    pallas_call x7 -> x8, Pallas kernels: 88.2 us -> 92.7 us  [dedisperse(): pl.pallas_call(functools.partial(dedisperse_kernel, chans=chans, each=eac...]
    all_to_all x7 -> x8, starting transfers between devices: 34.2 us -> 38.3 us  [send_volts(): lax.all_to_all(piece, 'feed', split_axis=0, concat_axis=0, axis_index_gro...]
    pallas_call x7 -> x8, Pallas kernels: 165 us -> 169 us  [partial_beams(): pl.pallas_call(functools.partial(partial_kernel, senders=senders, start=s...]
    ppermute x21 -> x24, starting transfers between devices: 25.2 us -> 28.7 us  [swapped(): return lax.ppermute(part, 'feed', [(j, j ^ step) for j in range(devices)])]
    pallas_call x7 -> x8, Pallas kernels: 19.8 us -> 22 us  [joined(): pl.pallas_call(functools.partial(joined_kernel, parts=len(parts)), grid_s...]
  transfers between devices with their start and end apart: 42 -> 48, of which waited for: 18 -> 18; matrix products, arithmetic and copies ran while one was open for 2% -> 2% of each run, Pallas kernels for 43% -> 45%
where the time goes in v3:
time: 739 us; the launch traced here: 729 us
  Pallas kernels  340 us (46%)
  waiting for transfers between devices  275 us (37%)
  starting transfers between devices  71.1 us (10%)
  other arithmetic  15.9 us (2%)
  between operations  14.1 us (2%)
  blocking collectives  8.58 us (1%)
    all_to_all x8, waiting for transfers between devices, send_volts(): lax.all_to_all(piece, 'feed', split_axis=0, concat_axis=0, axis_index_gro...  201 us
    pallas_call x8, Pallas kernels, partial_beams(): pl.pallas_call(functools.partial(partial_kernel, senders=senders, start=s...  169 us
    pallas_call x8, Pallas kernels, dedisperse(): pl.pallas_call(functools.partial(dedisperse_kernel, chans=chans, each=eac...  92.7 us
    ppermute x8, waiting for transfers between devices, form_partial(): came[i] = lax.ppermute(theirs[i], 'feed', opposite)  50.4 us
    all_to_all x8, starting transfers between devices, send_volts(): lax.all_to_all(piece, 'feed', split_axis=0, concat_axis=0, axis_index_gro...  38.3 us
    pallas_call x8, Pallas kernels, taken(): pl.pallas_call(taken_kernel, grid=(size // step,), in_specs=[pl.BlockSpec...  31 us
    ppermute x24, starting transfers between devices, swapped(): return lax.ppermute(part, 'feed', [(j, j ^ step) for j in range(devices)])  28.7 us
    pallas_call x8, Pallas kernels, beam_spectra(): pl.pallas_call(functools.partial(spectra_kernel, kc=kc, split_rows=split_...  25.4 us
  transfers between devices with their start and end apart: 48, of which 18 were waited for; matrix products, arithmetic and copies ran while one was open for 2% of the time, Pallas kernels for 45%

profile of v3, /device:TPU:0, one launch (start us, length us, event | category | flops | bytes accessed | tf_op | source)
XLA Modules:
  0.0 728.8 jit_solution(12732508402063205043)
XLA Ops:
  9.1 5.2 all-to-all-start.4
  15.1 4.8 taken.8
  23.2 8.6 %all-gather.1 = s32[768,256]{1,0:T(8,128)S(1)} all-gather(s32[192,256]{1,0:T(8,128)S(1)} %copy-done.1), channel_id=3, replica_groups=mesh['band'=4,'feed'=8] {'band'}, dimensions={0}, use_global_device_ids=true | all-gather | bytes 983040 | tf_op jit(solution)/shard_map/all_gather | solution.py:430
  34.1 6.4 fusion.9
  46.6 5.1 all-to-all-start
  51.7 15.3 %partial_beams.12 = (f32[2048,128]{1,0:T(8,128)}, f32[2048,128]{1,0:T(8,128)}) custom-call(s32[1024]{0:T(1024)} %dynamic_slice.6.cells_ref, f32[4,4,256,128]{3,2,1,0:T(8,128)} %bitcast.26, bf16[48,64,192]{2,1,0:T(8,128)(2,1)} %pad_maximum_fusion.1.refs_1_, bf16[48,64,192]{2,1,0:T(8,128)(2,1)} %pad_maximum_fusion.3.refs_2_), custom_call_target="tpu_custom_call" | custom-call | flops 155999993856 | tf_op jit(solution)/shard_map/partial_beams/pallas_call | solution.py:144
  69.6 4.8 taken.13
  74.4 48.4 %all-to-all-done = f32[32,256,128]{2,1,0:T(8,128)} async-done(((f32[32,256,128]{2,1,0:T(8,128)}), f32[32,256,128]{2,1,0:T(8,128)}, u32[]{:S(2)}, u32[]{:S(2)}) %all-to-all-start) | async-done | bytes 4194336 | tf_op jit(solution)/shard_map/all_to_all | solution.py:403
  122.7 4.9 all-to-all-start.5
  127.6 26.9 %partial_beams.8 = (f32[4096,128]{1,0:T(8,128)}, f32[4096,128]{1,0:T(8,128)}) custom-call(s32[1024]{0:T(1024)} %dynamic_slice.6.cells_ref, f32[4,8,256,128]{3,2,1,0:T(8,128)} %bitcast.refs_0_, bf16[48,64,192]{2,1,0:T(8,128)(2,1)} %pad_maximum_fusion.1.refs_1_, bf16[48,64,192]{2,1,0:T(8,128)(2,1)} %pad_maximum_fusion.3.refs_2_), custom_call_target="tpu_custom_call" | custom-call | flops 311999987712 | tf_op jit(solution)/shard_map/partial_beams/pallas_call | solution.py:144
  154.5 4.8 taken.9
  162.4 3.6 collective-permute-start.10
  166.6 22.4 %all-to-all-done.5 = f32[32,256,128]{2,1,0:T(8,128)} async-done(((f32[32,256,128]{2,1,0:T(8,128)}), f32[32,256,128]{2,1,0:T(8,128)}, u32[]{:S(2)}, u32[]{:S(2)}) %all-to-all-start.5) | async-done | bytes 4194336 | tf_op jit(solution)/shard_map/all_to_all | solution.py:403
  189.0 4.8 all-to-all-start.1
  193.9 26.8 %partial_beams.13 = (f32[4096,128]{1,0:T(8,128)}, f32[4096,128]{1,0:T(8,128)}) custom-call(s32[1024]{0:T(1024)} %dynamic_slice.6.cells_ref, f32[4,8,256,128]{3,2,1,0:T(8,128)} %bitcast.8.refs_0_, bf16[48,64,192]{2,1,0:T(8,128)(2,1)} %pad_maximum_fusion.1.refs_1_, bf16[48,64,192]{2,1,0:T(8,128)(2,1)} %pad_maximum_fusion.3.refs_2_), custom_call_target="tpu_custom_call" | custom-call | flops 311999987712 | tf_op jit(solution)/shard_map/partial_beams/pallas_call | solution.py:144
  220.7 4.8 taken.14
  228.1 26.0 %collective-permute-done.3.came_ref = f32[4096,128]{1,0:T(8,128)} collective-permute-done((f32[4096,128]{1,0:T(8,128)}, f32[4096,128]{1,0:T(8,128)}, u32[]{:S(2)}, u32[]{:S(2)}) %collective-permute-start.3) | collective-permute-done | bytes 2097184 | tf_op jit(solution)/shard_map/ppermute | solution.py:409
  254.1 3.4 beam_spectra.8
  261.1 32.2 %all-to-all-done.1 = f32[32,256,128]{2,1,0:T(8,128)} async-done(((f32[32,256,128]{2,1,0:T(8,128)}), f32[32,256,128]{2,1,0:T(8,128)}, u32[]{:S(2)}, u32[]{:S(2)}) %all-to-all-start.1) | async-done | bytes 4194336 | tf_op jit(solution)/shard_map/all_to_all | solution.py:403
  293.3 4.8 all-to-all-start.6
  298.6 26.8 %partial_beams.9 = (f32[4096,128]{1,0:T(8,128)}, f32[4096,128]{1,0:T(8,128)}) custom-call(s32[1024]{0:T(1024)} %dynamic_slice.6.cells_ref, f32[4,8,256,128]{3,2,1,0:T(8,128)} %bitcast.4.refs_0_, bf16[48,64,192]{2,1,0:T(8,128)(2,1)} %pad_maximum_fusion.1.refs_1_, bf16[48,64,192]{2,1,0:T(8,128)(2,1)} %pad_maximum_fusion.3.refs_2_), custom_call_target="tpu_custom_call" | custom-call | flops 311999987712 | tf_op jit(solution)/shard_map/partial_beams/pallas_call | solution.py:144
  325.4 4.4 taken.10
  329.8 9.2 %dedisperse.8.refs_4_.refs_1_ = f32[4096,128]{1,0:T(8,128)} custom-call(f32[4096,128]{1,0:T(8,128)} %bitcast.34, f32[4,192,64]{2,1,0:T(8,128)} %get-tuple-element.106.refs_1_, f32[4,192,64]{2,1,0:T(8,128)} %get-tuple-element.105.refs_2_, bf16[64,192]{1,0:T(8,128)(2,1)} %pad_maximum_fusion.6.refs_3_), custom_call_target="tpu_custom_call" | custom-call | flops 130000003072 | tf_op jit(solution)/shard_map/dedisperse/pallas_call | solution.py:336
  339.0 4.9 collective-permute-done.14.came_ref
  344.0 3.4 beam_spectra.11
  353.9 51.8 %all-to-all-done.6 = f32[32,256,128]{2,1,0:T(8,128)} async-done(((f32[32,256,128]{2,1,0:T(8,128)}), f32[32,256,128]{2,1,0:T(8,128)}, u32[]{:S(2)}, u32[]{:S(2)}) %all-to-all-start.6) | async-done | bytes 4194336 | tf_op jit(solution)/shard_map/all_to_all | solution.py:403
  405.7 4.7 all-to-all-start.2
  410.4 26.9 %partial_beams.14 = (f32[4096,128]{1,0:T(8,128)}, f32[4096,128]{1,0:T(8,128)}) custom-call(s32[1024]{0:T(1024)} %dynamic_slice.6.cells_ref, f32[4,8,256,128]{3,2,1,0:T(8,128)} %bitcast.9.refs_0_, bf16[48,64,192]{2,1,0:T(8,128)(2,1)} %pad_maximum_fusion.1.refs_1_, bf16[48,64,192]{2,1,0:T(8,128)(2,1)} %pad_maximum_fusion.3.refs_2_), custom_call_target="tpu_custom_call" | custom-call | flops 311999987712 | tf_op jit(solution)/shard_map/partial_beams/pallas_call | solution.py:144
  442.9 13.5 %dedisperse.9.refs_1_.refs_4_ = f32[4096,128]{1,0:T(8,128)} custom-call(f32[8192,128]{1,0:T(8,128)} %bitcast.31, f32[4,192,64]{2,1,0:T(8,128)} %get-tuple-element.106.refs_1_, f32[4,192,64]{2,1,0:T(8,128)} %get-tuple-element.105.refs_2_, bf16[64,192]{1,0:T(8,128)(2,1)} %pad_maximum_fusion.6.refs_3_, f32[4096,128]{1,0:T(8,128)} %dedisperse.8.refs_4_.refs_1_), custom_call_target="tpu_custom_call" | custom-call | flops 130000003072 | tf_op jit(solution)/shard_map/dedisperse/pallas_call | solution.py:336
  456.4 3.4 beam_spectra.10
  463.3 30.3 %all-to-all-done.2 = f32[24,256,128]{2,1,0:T(8,128)} async-done(((f32[24,256,128]{2,1,0:T(8,128)}), f32[24,256,128]{2,1,0:T(8,128)}, u32[]{:S(2)}, u32[]{:S(2)}) %all-to-all-start.2) | async-done | bytes 3145760 | tf_op jit(solution)/shard_map/all_to_all | solution.py:403
  493.6 4.4 all-to-all-start.7
  498.2 21.0 %partial_beams.10 = (f32[3072,128]{1,0:T(8,128)}, f32[3072,128]{1,0:T(8,128)}) custom-call(s32[1024]{0:T(1024)} %dynamic_slice.6.cells_ref, f32[4,6,256,128]{3,2,1,0:T(8,128)} %bitcast.5.refs_0_, bf16[48,64,192]{2,1,0:T(8,128)(2,1)} %pad_maximum_fusion.1.refs_1_, bf16[48,64,192]{2,1,0:T(8,128)(2,1)} %pad_maximum_fusion.3.refs_2_), custom_call_target="tpu_custom_call" | custom-call | flops 234000007168 | tf_op jit(solution)/shard_map/partial_beams/pallas_call | solution.py:144
  524.5 13.5 %dedisperse.10.refs_4_.refs_1_ = f32[4096,128]{1,0:T(8,128)} custom-call(f32[8192,128]{1,0:T(8,128)} %bitcast.29, f32[4,192,64]{2,1,0:T(8,128)} %get-tuple-element.106.refs_1_, f32[4,192,64]{2,1,0:T(8,128)} %get-tuple-element.105.refs_2_, bf16[64,192]{1,0:T(8,128)(2,1)} %pad_maximum_fusion.6.refs_3_, f32[4096,128]{1,0:T(8,128)} %dedisperse.9.refs_1_.refs_4_), custom_call_target="tpu_custom_call" | custom-call | flops 130000003072 | tf_op jit(solution)/shard_map/dedisperse/pallas_call | solution.py:336
  537.9 3.4 beam_spectra.13
  544.9 16.2 %all-to-all-done.7 = f32[16,256,128]{2,1,0:T(8,128)} async-done(((f32[16,256,128]{2,1,0:T(8,128)}), f32[16,256,128]{2,1,0:T(8,128)}, u32[]{:S(2)}, u32[]{:S(2)}) %all-to-all-start.7) | async-done | bytes 2097184 | tf_op jit(solution)/shard_map/all_to_all | solution.py:403
  561.0 4.3 all-to-all-start.3
  565.4 15.3 %partial_beams.15 = (f32[2048,128]{1,0:T(8,128)}, f32[2048,128]{1,0:T(8,128)}) custom-call(s32[1024]{0:T(1024)} %dynamic_slice.6.cells_ref, f32[4,4,256,128]{3,2,1,0:T(8,128)} %bitcast.10.refs_0_, bf16[48,64,192]{2,1,0:T(8,128)(2,1)} %pad_maximum_fusion.1.refs_1_, bf16[48,64,192]{2,1,0:T(8,128)(2,1)} %pad_maximum_fusion.3.refs_2_), custom_call_target="tpu_custom_call" | custom-call | flops 155999993856 | tf_op jit(solution)/shard_map/partial_beams/pallas_call | solution.py:144
  580.6 3.7 collective-permute-done.24.refs_3_
  587.3 13.4 %dedisperse.11.refs_1_.refs_4_ = f32[4096,128]{1,0:T(8,128)} custom-call(f32[8192,128]{1,0:T(8,128)} %bitcast.28, f32[4,192,64]{2,1,0:T(8,128)} %get-tuple-element.106.refs_1_, f32[4,192,64]{2,1,0:T(8,128)} %get-tuple-element.105.refs_2_, bf16[64,192]{1,0:T(8,128)(2,1)} %pad_maximum_fusion.6.refs_3_, f32[4096,128]{1,0:T(8,128)} %dedisperse.10.refs_4_.refs_1_), custom_call_target="tpu_custom_call" | custom-call | flops 130000003072 | tf_op jit(solution)/shard_map/dedisperse/pallas_call | solution.py:336
  600.8 19.5 %collective-permute-done.1.came_ref = f32[3072,128]{1,0:T(8,128)} collective-permute-done((f32[3072,128]{1,0:T(8,128)}, f32[3072,128]{1,0:T(8,128)}, u32[]{:S(2)}, u32[]{:S(2)}) %collective-permute-start.1) | collective-permute-done | bytes 1572896 | tf_op jit(solution)/shard_map/ppermute | solution.py:409
  620.2 3.9 beam_spectra.12
  627.6 9.8 %partial_beams.11 = (f32[1024,128]{1,0:T(8,128)}, f32[1024,128]{1,0:T(8,128)}) custom-call(s32[1024]{0:T(1024)} %dynamic_slice.6.cells_ref, f32[4,2,256,128]{3,2,1,0:T(8,128)} %bitcast.6.refs_0_, bf16[48,64,192]{2,1,0:T(8,128)(2,1)} %pad_maximum_fusion.1.refs_1_, bf16[48,64,192]{2,1,0:T(8,128)(2,1)} %pad_maximum_fusion.3.refs_2_), custom_call_target="tpu_custom_call" | custom-call | flops 77999996928 | tf_op jit(solution)/shard_map/partial_beams/pallas_call | solution.py:144
  646.0 13.5 %dedisperse.12.refs_4_.refs_1_ = f32[4096,128]{1,0:T(8,128)} custom-call(f32[8192,128]{1,0:T(8,128)} %bitcast.30, f32[4,192,64]{2,1,0:T(8,128)} %get-tuple-element.106.refs_1_, f32[4,192,64]{2,1,0:T(8,128)} %get-tuple-element.105.refs_2_, bf16[64,192]{1,0:T(8,128)(2,1)} %pad_maximum_fusion.6.refs_3_, f32[4096,128]{1,0:T(8,128)} %dedisperse.11.refs_1_.refs_4_), custom_call_target="tpu_custom_call" | custom-call | flops 130000003072 | tf_op jit(solution)/shard_map/dedisperse/pallas_call | solution.py:336
  673.9 12.0 %dedisperse.13.refs_0_.refs_4_ = f32[4096,128]{1,0:T(8,128)} custom-call(f32[6144,128]{1,0:T(8,128)} %bitcast.32, f32[4,192,64]{2,1,0:T(8,128)} %get-tuple-element.106.refs_1_, f32[4,192,64]{2,1,0:T(8,128)} %get-tuple-element.105.refs_2_, bf16[64,192]{1,0:T(8,128)(2,1)} %pad_maximum_fusion.6.refs_3_, f32[4096,128]{1,0:T(8,128)} %dedisperse.12.refs_4_.refs_1_), custom_call_target="tpu_custom_call" | custom-call | flops 130000003072 | tf_op jit(solution)/shard_map/dedisperse/pallas_call | solution.py:336
  698.5 10.0 %dedisperse.14.refs_4_ = f32[4096,128]{1,0:T(8,128)} custom-call(f32[4096,128]{1,0:T(8,128)} %bitcast.33, f32[4,192,64]{2,1,0:T(8,128)} %get-tuple-element.106.refs_1_, f32[4,192,64]{2,1,0:T(8,128)} %get-tuple-element.105.refs_2_, bf16[64,192]{1,0:T(8,128)(2,1)} %pad_maximum_fusion.6.refs_3_, f32[4096,128]{1,0:T(8,128)} %dedisperse.13.refs_0_.refs_4_), custom_call_target="tpu_custom_call" | custom-call | flops 130000003072 | tf_op jit(solution)/shard_map/dedisperse/pallas_call | solution.py:336
  708.5 5.6 all-gather.30.cloned.1.call-done
  714.1 7.6 %dedisperse.15 = f32[4096,128]{1,0:T(8,128)} custom-call(f32[2048,128]{1,0:T(8,128)} %bitcast.35, f32[4,192,64]{2,1,0:T(8,128)} %get-tuple-element.106.refs_1_, f32[4,192,64]{2,1,0:T(8,128)} %get-tuple-element.105.refs_2_, bf16[64,192]{1,0:T(8,128)(2,1)} %pad_maximum_fusion.6.refs_3_, f32[4096,128]{1,0:T(8,128)} %dedisperse.14.refs_4_), custom_call_target="tpu_custom_call" | custom-call | flops 130000003072 | tf_op jit(solution)/shard_map/dedisperse/pallas_call | solution.py:336
  (156 shorter events, 94.5 us)
Async XLA Ops:
  9.1 36.1 %all-to-all-start.4 = ((f32[16,256,128]{2,1,0:T(8,128)}), f32[16,256,128]{2,1,0:T(8,128)S(1)}, u32[]{:S(2)}, u32[]{:S(2)}) async-start(f32[16,256,128]{2,1,0:T(8,128)} %taken.12), calls=%async_computation.4 | async-start | bytes 4194304 | tf_op jit(solution)/shard_map/all_to_all | solution.py:403
  46.6 76.1 %all-to-all-start = ((f32[32,256,128]{2,1,0:T(8,128)}), f32[32,256,128]{2,1,0:T(8,128)}, u32[]{:S(2)}, u32[]{:S(2)}) async-start(f32[32,256,128]{2,1,0:T(8,128)} %taken.8), calls=%async_computation | async-start | bytes 8388608 | tf_op jit(solution)/shard_map/all_to_all | solution.py:403
  67.0 92.7 %collective-permute-start.7 = (f32[2048,128]{1,0:T(8,128)}, f32[2048,128]{1,0:T(8,128)}, u32[]{:S(2)}, u32[]{:S(2)}) collective-permute-start(f32[2048,128]{1,0:T(8,128)} %get-tuple-element.59.refs_1_), channel_id=1, source_target_pairs={{0,4},{1,5},{2,6},{3,7},{4,0},{5,1},{6,2},{7,3},{8,12},{9,13},{10,... | collective-permute-start | bytes 3145736 | tf_op jit(solution)/shard_map/ppermute | solution.py:409
  122.7 66.3 %all-to-all-start.5 = ((f32[32,256,128]{2,1,0:T(8,128)}), f32[32,256,128]{2,1,0:T(8,128)}, u32[]{:S(2)}, u32[]{:S(2)}) async-start(f32[32,256,128]{2,1,0:T(8,128)} %taken.13), calls=%async_computation.5 | async-start | bytes 8388608 | tf_op jit(solution)/shard_map/all_to_all | solution.py:403
  159.3 94.8 %collective-permute-start.3 = (f32[4096,128]{1,0:T(8,128)}, f32[4096,128]{1,0:T(8,128)}, u32[]{:S(2)}, u32[]{:S(2)}) collective-permute-start(f32[4096,128]{1,0:T(8,128)} %get-tuple-element.53.refs_1_.refs_0_), channel_id=1, source_target_pairs={{0,4},{1,5},{2,6},{3,7},{4,0},{5,1},{6,2},{7,3},{8,12},{9,13},{10,... | collective-permute-start | bytes 6291464 | tf_op jit(solution)/shard_map/ppermute | solution.py:409
  162.4 63.0 %collective-permute-start.10 = (f32[4,64,128]{2,1,0:T(8,128)}, f32[4,64,128]{2,1,0:T(8,128)}, u32[]{:S(2)}, u32[]{:S(2)}) collective-permute-start(f32[4,64,128]{2,1,0:T(8,128)} %get-tuple-element.73), channel_id=1, source_target_pairs={{0,3},{1,2},{2,1},{3,0},{4,7},{5,6},{6,5},{7,4},{8,11},{9,10},{10,... | collective-permute-start | bytes 393224 | tf_op jit(solution)/shard_map/ppermute | solution.py:393
  166.0 59.4 %collective-permute-start.8 = (f32[4,64,128]{2,1,0:T(8,128)}, f32[4,64,128]{2,1,0:T(8,128)}, u32[]{:S(2)}, u32[]{:S(2)}) collective-permute-start(f32[4,64,128]{2,1,0:T(8,128)} %get-tuple-element.71), channel_id=1, source_target_pairs={{0,1},{1,0},{2,3},{3,2},{4,5},{5,4},{6,7},{7,6},{8,9},{9,8},{10,11... | collective-permute-start | bytes 393224 | tf_op jit(solution)/shard_map/ppermute | solution.py:393
  166.0 59.4 %collective-permute-start.9 = (f32[4,64,128]{2,1,0:T(8,128)}, f32[4,64,128]{2,1,0:T(8,128)}, u32[]{:S(2)}, u32[]{:S(2)}) collective-permute-start(f32[4,64,128]{2,1,0:T(8,128)} %get-tuple-element.72), channel_id=1, source_target_pairs={{0,2},{1,3},{2,0},{3,1},{4,6},{5,7},{6,4},{7,5},{8,10},{9,11},{10,... | collective-permute-start | bytes 393224 | tf_op jit(solution)/shard_map/ppermute | solution.py:393
  189.0 104.2 %all-to-all-start.1 = ((f32[32,256,128]{2,1,0:T(8,128)}), f32[32,256,128]{2,1,0:T(8,128)}, u32[]{:S(2)}, u32[]{:S(2)}) async-start(f32[32,256,128]{2,1,0:T(8,128)} %taken.9), calls=%async_computation.1 | async-start | bytes 8388608 | tf_op jit(solution)/shard_map/all_to_all | solution.py:403
  193.9 136.0 %all-gather.20.cloned.1.call-start = ((), (), s32[]{:S(2)}) async-start(), calls=%async_computation.9 | async-start | bytes 2621440 | tf_op jit(solution)/shard_map/all_gather | solution.py:416
  220.7 123.3 %collective-permute-start.14 = (f32[4096,128]{1,0:T(8,128)}, f32[4096,128]{1,0:T(8,128)}, u32[]{:S(2)}, u32[]{:S(2)}) collective-permute-start(f32[4096,128]{1,0:T(8,128)} %get-tuple-element.60.refs_1_.refs_0_.refs_4_), channel_id=1, source_target_pairs={{0,4},{1,5},{2,6},{3,7},{4,0},{5,1},{6,2},{7,3},{8,12},{9,13},{10,... | collective-permute-start | bytes 6291464 | tf_op jit(solution)/shard_map/ppermute | solution.py:409
  257.5 91.9 %collective-permute-start.4 = (f32[8,64,128]{2,1,0:T(8,128)}, f32[8,64,128]{2,1,0:T(8,128)}, u32[]{:S(2)}, u32[]{:S(2)}) collective-permute-start(f32[8,64,128]{2,1,0:T(8,128)} %get-tuple-element.66), channel_id=1, source_target_pairs={{0,1},{1,0},{2,3},{3,2},{4,5},{5,4},{6,7},{7,6},{8,9},{9,8},{10,11... | collective-permute-start | bytes 786440 | tf_op jit(solution)/shard_map/ppermute | solution.py:393
  259.5 89.9 %collective-permute-start.5 = (f32[8,64,128]{2,1,0:T(8,128)}, f32[8,64,128]{2,1,0:T(8,128)}, u32[]{:S(2)}, u32[]{:S(2)}) collective-permute-start(f32[8,64,128]{2,1,0:T(8,128)} %get-tuple-element.67), channel_id=1, source_target_pairs={{0,2},{1,3},{2,0},{3,1},{4,6},{5,7},{6,4},{7,5},{8,10},{9,11},{10,... | collective-permute-start | bytes 786440 | tf_op jit(solution)/shard_map/ppermute | solution.py:393
  259.5 91.5 %collective-permute-start.6 = (f32[8,64,128]{2,1,0:T(8,128)}, f32[8,64,128]{2,1,0:T(8,128)}, u32[]{:S(2)}, u32[]{:S(2)}) collective-permute-start(f32[8,64,128]{2,1,0:T(8,128)} %get-tuple-element.68), channel_id=1, source_target_pairs={{0,3},{1,2},{2,1},{3,0},{4,7},{5,6},{6,5},{7,4},{8,11},{9,10},{10,... | collective-permute-start | bytes 786440 | tf_op jit(solution)/shard_map/ppermute | solution.py:393
  293.3 112.4 %all-to-all-start.6 = ((f32[32,256,128]{2,1,0:T(8,128)}), f32[32,256,128]{2,1,0:T(8,128)}, u32[]{:S(2)}, u32[]{:S(2)}) async-start(f32[32,256,128]{2,1,0:T(8,128)} %taken.14), calls=%async_computation.6 | async-start | bytes 8388608 | tf_op jit(solution)/shard_map/all_to_all | solution.py:403
  298.1 144.8 %all-gather.18.cloned.1.call-start = ((), (), s32[]{:S(2)}) async-start(), calls=%async_computation.8 | async-start | bytes 5242880 | tf_op jit(solution)/shard_map/all_gather | solution.py:416
  329.8 126.5 %collective-permute-start.2 = (f32[4096,128]{1,0:T(8,128)}, f32[4096,128]{1,0:T(8,128)}, u32[]{:S(2)}, u32[]{:S(2)}) collective-permute-start(f32[4096,128]{1,0:T(8,128)} %get-tuple-element.54.refs_1_.refs_4_.refs_0_), channel_id=1, source_target_pairs={{0,4},{1,5},{2,6},{3,7},{4,0},{5,1},{6,2},{7,3},{8,12},{9,13},{10,... | collective-permute-start | bytes 6291464 | tf_op jit(solution)/shard_map/ppermute | solution.py:409
  347.4 92.5 %collective-permute-start.15 = (f32[8,64,128]{2,1,0:T(8,128)}, f32[8,64,128]{2,1,0:T(8,128)}, u32[]{:S(2)}, u32[]{:S(2)}) collective-permute-start(f32[8,64,128]{2,1,0:T(8,128)} %get-tuple-element.80), channel_id=1, source_target_pairs={{0,1},{1,0},{2,3},{3,2},{4,5},{5,4},{6,7},{7,6},{8,9},{9,8},{10,11... | collective-permute-start | bytes 786440 | tf_op jit(solution)/shard_map/ppermute | solution.py:393
  349.4 90.5 %collective-permute-start.16 = (f32[8,64,128]{2,1,0:T(8,128)}, f32[8,64,128]{2,1,0:T(8,128)}, u32[]{:S(2)}, u32[]{:S(2)}) collective-permute-start(f32[8,64,128]{2,1,0:T(8,128)} %get-tuple-element.81), channel_id=1, source_target_pairs={{0,2},{1,3},{2,0},{3,1},{4,6},{5,7},{6,4},{7,5},{8,10},{9,11},{10,... | collective-permute-start | bytes 786440 | tf_op jit(solution)/shard_map/ppermute | solution.py:393
  349.5 90.5 %collective-permute-start.17 = (f32[8,64,128]{2,1,0:T(8,128)}, f32[8,64,128]{2,1,0:T(8,128)}, u32[]{:S(2)}, u32[]{:S(2)}) collective-permute-start(f32[8,64,128]{2,1,0:T(8,128)} %get-tuple-element.82), channel_id=1, source_target_pairs={{0,3},{1,2},{2,1},{3,0},{4,7},{5,6},{6,5},{7,4},{8,11},{9,10},{10,... | collective-permute-start | bytes 786440 | tf_op jit(solution)/shard_map/ppermute | solution.py:393
  405.7 87.9 %all-to-all-start.2 = ((f32[24,256,128]{2,1,0:T(8,128)}), f32[24,256,128]{2,1,0:T(8,128)}, u32[]{:S(2)}, u32[]{:S(2)}) async-start(f32[24,256,128]{2,1,0:T(8,128)} %taken.10), calls=%async_computation.2 | async-start | bytes 6291456 | tf_op jit(solution)/shard_map/all_to_all | solution.py:403
  410.4 114.1 %all-gather.24.cloned.1.call-start = ((), (), s32[]{:S(2)}) async-start(), calls=%async_computation.11 | async-start | bytes 5242880 | tf_op jit(solution)/shard_map/all_gather | solution.py:416
  437.3 100.7 %collective-permute-start.21 = (f32[4096,128]{1,0:T(8,128)}, f32[4096,128]{1,0:T(8,128)}, u32[]{:S(2)}, u32[]{:S(2)}) collective-permute-start(f32[4096,128]{1,0:T(8,128)} %get-tuple-element.61.refs_1_.refs_0_.refs_4_), channel_id=1, source_target_pairs={{0,4},{1,5},{2,6},{3,7},{4,0},{5,1},{6,2},{7,3},{8,12},{9,13},{10,... | collective-permute-start | bytes 6291464 | tf_op jit(solution)/shard_map/ppermute | solution.py:409
  459.8 61.7 %collective-permute-start.11 = (f32[8,64,128]{2,1,0:T(8,128)}, f32[8,64,128]{2,1,0:T(8,128)}, u32[]{:S(2)}, u32[]{:S(2)}) collective-permute-start(f32[8,64,128]{2,1,0:T(8,128)} %get-tuple-element.75), channel_id=1, source_target_pairs={{0,1},{1,0},{2,3},{3,2},{4,5},{5,4},{6,7},{7,6},{8,9},{9,8},{10,11... | collective-permute-start | bytes 786440 | tf_op jit(solution)/shard_map/ppermute | solution.py:393
  461.7 59.8 %collective-permute-start.12 = (f32[8,64,128]{2,1,0:T(8,128)}, f32[8,64,128]{2,1,0:T(8,128)}, u32[]{:S(2)}, u32[]{:S(2)}) collective-permute-start(f32[8,64,128]{2,1,0:T(8,128)} %get-tuple-element.76), channel_id=1, source_target_pairs={{0,2},{1,3},{2,0},{3,1},{4,6},{5,7},{6,4},{7,5},{8,10},{9,11},{10,... | collective-permute-start | bytes 786440 | tf_op jit(solution)/shard_map/ppermute | solution.py:393
  463.2 58.3 %collective-permute-start.13 = (f32[8,64,128]{2,1,0:T(8,128)}, f32[8,64,128]{2,1,0:T(8,128)}, u32[]{:S(2)}, u32[]{:S(2)}) collective-permute-start(f32[8,64,128]{2,1,0:T(8,128)} %get-tuple-element.77), channel_id=1, source_target_pairs={{0,3},{1,2},{2,1},{3,0},{4,7},{5,6},{6,5},{7,4},{8,11},{9,10},{10,... | collective-permute-start | bytes 786440 | tf_op jit(solution)/shard_map/ppermute | solution.py:393
  493.6 67.5 %all-to-all-start.7 = ((f32[16,256,128]{2,1,0:T(8,128)}), f32[16,256,128]{2,1,0:T(8,128)}, u32[]{:S(2)}, u32[]{:S(2)}) async-start(f32[16,256,128]{2,1,0:T(8,128)} %taken.15), calls=%async_computation.7 | async-start | bytes 4194304 | tf_op jit(solution)/shard_map/all_to_all | solution.py:403
  498.0 89.3 %all-gather.22.cloned.1.call-start = ((), (), s32[]{:S(2)}) async-start(), calls=%async_computation.10 | async-start | bytes 5242880 | tf_op jit(solution)/shard_map/all_gather | solution.py:416
  521.5 98.7 %collective-permute-start.1 = (f32[3072,128]{1,0:T(8,128)}, f32[3072,128]{1,0:T(8,128)}, u32[]{:S(2)}, u32[]{:S(2)}) collective-permute-start(f32[3072,128]{1,0:T(8,128)} %get-tuple-element.55.refs_1_.refs_4_.refs_0_), channel_id=1, source_target_pairs={{0,4},{1,5},{2,6},{3,7},{4,0},{5,1},{6,2},{7,3},{8,12},{9,13},{10,... | collective-permute-start | bytes 4718600 | tf_op jit(solution)/shard_map/ppermute | solution.py:409
  541.4 39.2 %collective-permute-start.22 = (f32[8,64,128]{2,1,0:T(8,128)}, f32[8,64,128]{2,1,0:T(8,128)}, u32[]{:S(2)}, u32[]{:S(2)}) collective-permute-start(f32[8,64,128]{2,1,0:T(8,128)} %get-tuple-element.89), channel_id=1, source_target_pairs={{0,1},{1,0},{2,3},{3,2},{4,5},{5,4},{6,7},{7,6},{8,9},{9,8},{10,11... | collective-permute-start | bytes 786440 | tf_op jit(solution)/shard_map/ppermute | solution.py:393
  543.3 37.3 %collective-permute-start.23 = (f32[8,64,128]{2,1,0:T(8,128)}, f32[8,64,128]{2,1,0:T(8,128)}, u32[]{:S(2)}, u32[]{:S(2)}) collective-permute-start(f32[8,64,128]{2,1,0:T(8,128)} %get-tuple-element.90), channel_id=1, source_target_pairs={{0,2},{1,3},{2,0},{3,1},{4,6},{5,7},{6,4},{7,5},{8,10},{9,11},{10,... | collective-permute-start | bytes 786440 | tf_op jit(solution)/shard_map/ppermute | solution.py:393
  544.8 39.5 %collective-permute-start.24 = (f32[8,64,128]{2,1,0:T(8,128)}, f32[8,64,128]{2,1,0:T(8,128)}, u32[]{:S(2)}, u32[]{:S(2)}) collective-permute-start(f32[8,64,128]{2,1,0:T(8,128)} %get-tuple-element.91), channel_id=1, source_target_pairs={{0,3},{1,2},{2,1},{3,0},{4,7},{5,6},{6,5},{7,4},{8,11},{9,10},{10,... | collective-permute-start | bytes 786440 | tf_op jit(solution)/shard_map/ppermute | solution.py:393
  561.0 66.6 %all-to-all-start.3 = ((f32[8,256,128]{2,1,0:T(8,128)}), f32[8,256,128]{2,1,0:T(8,128)}, u32[]{:S(2)}, u32[]{:S(2)}) async-start(f32[8,256,128]{2,1,0:T(8,128)} %taken.11), calls=%async_computation.3 | async-start | bytes 2097152 | tf_op jit(solution)/shard_map/all_to_all | solution.py:403
  565.3 80.6 %all-gather.28.cloned.1.call-start = ((), (), s32[]{:S(2)}) async-start(), calls=%async_computation.13 | async-start | bytes 5242880 | tf_op jit(solution)/shard_map/all_gather | solution.py:416
  580.6 78.9 %collective-permute-start.28 = (f32[2048,128]{1,0:T(8,128)}, f32[2048,128]{1,0:T(8,128)}, u32[]{:S(2)}, u32[]{:S(2)}) collective-permute-start(f32[2048,128]{1,0:T(8,128)} %get-tuple-element.62.refs_0_.refs_4_), channel_id=1, source_target_pairs={{0,4},{1,5},{2,6},{3,7},{4,0},{5,1},{6,2},{7,3},{8,12},{9,13},{10,... | collective-permute-start | bytes 3145736 | tf_op jit(solution)/shard_map/ppermute | solution.py:409
  587.2 86.7 %all-gather.26.cloned.1.call-start = ((), (), s32[]{:S(2)}) async-start(), calls=%async_computation.12 | async-start | bytes 3932160 | tf_op jit(solution)/shard_map/all_gather | solution.py:416
  624.1 13.3 %collective-permute-start.18 = (f32[6,64,128]{2,1,0:T(8,128)}, f32[6,64,128]{2,1,0:T(8,128)S(1)}, u32[]{:S(2)}, u32[]{:S(2)}) collective-permute-start(f32[6,64,128]{2,1,0:T(8,128)} %get-tuple-element.84), channel_id=1, source_target_pairs={{0,1},{1,0},{2,3},{3,2},{4,5},{5,4},{6,7},{7,6},{8,9},{9,8},{10,11... | collective-permute-start | bytes 589832 | tf_op jit(solution)/shard_map/ppermute | solution.py:393
  625.4 13.7 %collective-permute-start.19 = (f32[6,64,128]{2,1,0:T(8,128)}, f32[6,64,128]{2,1,0:T(8,128)S(1)}, u32[]{:S(2)}, u32[]{:S(2)}) collective-permute-start(f32[6,64,128]{2,1,0:T(8,128)} %get-tuple-element.85), channel_id=1, source_target_pairs={{0,2},{1,3},{2,0},{3,1},{4,6},{5,7},{6,4},{7,5},{8,10},{9,11},{10,... | collective-permute-start | bytes 589832 | tf_op jit(solution)/shard_map/ppermute | solution.py:393
  625.4 16.9 %collective-permute-start.20 = (f32[6,64,128]{2,1,0:T(8,128)}, f32[6,64,128]{2,1,0:T(8,128)S(1)}, u32[]{:S(2)}, u32[]{:S(2)}) collective-permute-start(f32[6,64,128]{2,1,0:T(8,128)} %get-tuple-element.86), channel_id=1, source_target_pairs={{0,3},{1,2},{2,1},{3,0},{4,7},{5,6},{6,5},{7,4},{8,11},{9,10},{10,... | collective-permute-start | bytes 589832 | tf_op jit(solution)/shard_map/ppermute | solution.py:393
  645.9 52.6 %all-gather.32.cloned.1.call-start = ((), (), s32[]{:S(2)}) async-start(), calls=%async_computation.15 | async-start | bytes 2621440 | tf_op jit(solution)/shard_map/all_gather | solution.py:416
  662.3 5.2 collective-permute-start.29
  662.6 5.2 collective-permute-start.30
  662.6 7.8 %collective-permute-start.31 = (f32[4,64,128]{2,1,0:T(8,128)}, f32[4,64,128]{2,1,0:T(8,128)S(1)}, u32[]{:S(2)}, u32[]{:S(2)}) collective-permute-start(f32[4,64,128]{2,1,0:T(8,128)} %get-tuple-element.100), channel_id=1, source_target_pairs={{0,3},{1,2},{2,1},{3,0},{4,7},{5,6},{6,5},{7,4},{8,11},{9,10},{10,... | collective-permute-start | bytes 393224 | tf_op jit(solution)/shard_map/ppermute | solution.py:393
  665.8 20.1 %collective-permute-start = (f32[1024,128]{1,0:T(8,128)}, f32[1024,128]{1,0:T(8,128)}, u32[]{:S(2)}, u32[]{:S(2)}) collective-permute-start(f32[1024,128]{1,0:T(8,128)} %get-tuple-element.57.refs_4_.refs_0_), channel_id=1, source_target_pairs={{0,4},{1,5},{2,6},{3,7},{4,0},{5,1},{6,2},{7,3},{8,12},{9,13},{10,... | collective-permute-start | bytes 1572872 | tf_op jit(solution)/shard_map/ppermute | solution.py:409
  673.6 40.5 %all-gather.30.cloned.1.call-start = ((), (), s32[]{:S(2)}) async-start(), calls=%async_computation.14 | async-start | bytes 1310720 | tf_op jit(solution)/shard_map/all_gather | solution.py:416
  688.1 5.2 collective-permute-start.25
  688.4 4.9 collective-permute-start.26
  690.2 5.4 collective-permute-start.27
  (12 other events, 34.5 us)
Sparse Core Ops, SparseCore 0:
  228.2 24.1 all-gather.19
  354.1 33.6 all-gather.17
  443.0 36.0 all-gather.23
  524.6 36.1 all-gather.21
  587.3 34.7 all-gather.27
  646.0 25.4 all-gather.25
  673.7 21.9 all-gather.31
  698.6 15.4 all-gather.29
